TPU v7x, 128 devices: a whole 4x4x4 slice. The times are simulated.
128 devices in a mesh: lat: 8 (over x, z_lo), lon: 8 (over y, core), tp: 2 (over z_hi).
Axes of the slice: x: 4, y: 4, z: 4 (z_hi: 2, z_lo: 2; z = z_hi * 2 + z_lo), core: 2. Of those that a mesh axis runs over, the one named last changes fastest.
Arguments:
- tokens: bfloat16 [4, 48, 192, 1024], P(None, 'lat', 'lon', 'tp'), may hold values from -6 to 6
- w_qkv: bfloat16 [1024, 3, 1024], P(None, None, 'tp'), may hold values from -0.1875 to 0.1875
- w_proj: bfloat16 [1024, 1024], P(None, 'tp'), may hold values from -0.1875 to 0.1875
- bias_table: float32 [759, 16], P(None, 'tp'), may hold values from -4 to 4
- bias_index: int32 [144, 144], replicated, may hold values from 0 to 758
- regions: int32 [4, 48, 192], P(None, 'lat', 'lon'), may hold values from 0 to 8, as said below
- out_grad: bfloat16 [4, 48, 192, 1024], P(None, 'lat', 'lon', 'tp'), may hold values from -6 to 6
Outputs:
- grad_tokens: bfloat16 [4, 48, 192, 1024], P(None, 'lat', 'lon', 'tp')
- qkv_grad: float32 [1024, 3, 1024], P(('lat', 'lon'), None, 'tp')
- proj_grad: float32 [1024, 1024], P(('lat', 'lon'), 'tp')
Inputs may be any that keep to these rules, and one draw needn't show every extreme that they name: `regions`: region ids in the shifted frame follow the shifted-window layout: levels split into the blocks [0, 2), [2, 3), [3, 4) and latitude rows into [0, 42), [42, 45), [45, 48); the id is constant on each of the nine combinations of a level block and a row block, for all longitudes; every id is 0 or 8, and ids of different blocks may coincide. `bias_index`: entries of bias_table's first dimension.
All inputs are finite; a program needn't handle non-finite values.
Results may differ from a plain program's by a relative error of at most 0.014.
Values may be sent and summed in bfloat16 or wider, within the bound.
A program may use at most 128 MiB of HBM per device.

v0:
```python
import jax
import jax.numpy as jnp
from jax import lax
from jax.sharding import PartitionSpec as P

HD = 64
WL = 2
WA = 6
WB = 12


def from_behind(value, axis, by):
    devices = lax.axis_size(axis)
    return lax.ppermute(value, axis, [(i, (i + by) % devices) for i in range(devices)])


def to_windows(values):
    levels, row_count, col_count, feat_count = values.shape
    values = values.reshape(levels // WL, WL, row_count // WA, WA, col_count // WB, WB, feat_count)
    values = values.transpose(0, 2, 4, 1, 3, 5, 6)
    return values.reshape(-1, WL * WA * WB, feat_count)


def from_windows(values, levels, row_count, col_count):
    feat_count = values.shape[-1]
    values = values.reshape(levels // WL, row_count // WA, col_count // WB, WL, WA, WB, feat_count)
    values = values.transpose(0, 3, 1, 4, 2, 5, 6)
    return values.reshape(levels, row_count, col_count, feat_count)


def attention_grads(shifted_in, shifted_grad, regions, w_qkv, w_proj, bias_table, bias_index):
    levels, row_count, col_count, model_width = shifted_in.shape
    inner_width = w_qkv.shape[2]
    head_count = inner_width // HD
    cell_count = levels * row_count * col_count
    scale = HD ** (-0.5)
    flat_in = shifted_in.reshape(cell_count, model_width).astype(jnp.float32)
    center = jnp.mean(flat_in, axis=1, keepdims=True)
    spread = jnp.mean(jnp.square(flat_in - center), axis=1, keepdims=True)
    inv_std = lax.rsqrt(spread + 1e-05)
    normed = (flat_in - center) * inv_std
    normed_bf = normed.astype(jnp.bfloat16)
    qkv_flat = jnp.dot(
        normed_bf, w_qkv.reshape(model_width, 3 * inner_width), preferred_element_type=jnp.float32
    ).astype(jnp.bfloat16)
    qkv_win = to_windows(qkv_flat.reshape(levels, row_count, col_count, 3 * inner_width))
    count_win, window = (qkv_win.shape[0], qkv_win.shape[1])
    split_heads = qkv_win.reshape(count_win, window, 3, head_count, HD).transpose(2, 0, 3, 1, 4)
    queries, key_part, value_part = (split_heads[0], split_heads[1], split_heads[2])
    table_bias = jnp.take(bias_table, bias_index, axis=0).transpose(2, 0, 1)
    region_win = to_windows(regions[..., None])[..., 0]
    allowed = (region_win[:, :, None] == region_win[:, None, :])[:, None]
    scores = (
        jnp.einsum("whid,whjd->whij", queries, key_part, preferred_element_type=jnp.float32) * scale
        + table_bias
    )
    exp_scores = jnp.where(allowed, jnp.exp(scores), 0.0)
    attn_probs = exp_scores / jnp.sum(exp_scores, axis=-1, keepdims=True)
    probs_bf = attn_probs.astype(jnp.bfloat16)
    attended = jnp.einsum(
        "whij,whjd->whid", probs_bf, value_part, preferred_element_type=jnp.float32
    ).astype(jnp.bfloat16)
    attended_flat = from_windows(
        attended.transpose(0, 2, 1, 3).reshape(count_win, window, inner_width),
        levels,
        row_count,
        col_count,
    ).reshape(cell_count, inner_width)
    grad_flat = shifted_grad.reshape(cell_count, model_width)
    grad_attn = jnp.dot(grad_flat, w_proj, preferred_element_type=jnp.float32).astype(jnp.bfloat16)
    grad_win = to_windows(grad_attn.reshape(levels, row_count, col_count, inner_width))
    grad_win = grad_win.reshape(count_win, window, head_count, HD).transpose(0, 2, 1, 3)
    grad_probs = jnp.einsum(
        "whid,whjd->whij", grad_win, value_part, preferred_element_type=jnp.float32
    )
    grad_value = jnp.einsum(
        "whij,whid->whjd", probs_bf, grad_win, preferred_element_type=jnp.float32
    ).astype(jnp.bfloat16)
    grad_scores = (
        attn_probs * (grad_probs - jnp.sum(attn_probs * grad_probs, axis=-1, keepdims=True)) * scale
    ).astype(jnp.bfloat16)
    grad_query = jnp.einsum(
        "whij,whjd->whid", grad_scores, key_part, preferred_element_type=jnp.float32
    ).astype(jnp.bfloat16)
    grad_key = jnp.einsum(
        "whij,whid->whjd", grad_scores, queries, preferred_element_type=jnp.float32
    ).astype(jnp.bfloat16)
    stacked = jnp.stack([grad_query, grad_key, grad_value], axis=2)
    stacked = stacked.transpose(0, 3, 2, 1, 4).reshape(count_win, window, 3 * inner_width)
    grad_qkv = from_windows(stacked, levels, row_count, col_count).reshape(
        cell_count, 3 * inner_width
    )
    return (normed, inv_std, normed_bf, grad_qkv, grad_flat, attended_flat)


def roll_lat(stacked, direction):
    rim_width = WA // 2
    extent = stacked.shape[2]
    outgoing = stacked[:, :, :rim_width] if direction < 0 else stacked[:, :, extent - rim_width :]
    incoming = from_behind(outgoing, "lat", direction)
    if direction < 0:
        return jnp.concatenate([stacked[:, :, rim_width:], incoming], axis=2)
    return jnp.concatenate([incoming, stacked[:, :, : extent - rim_width]], axis=2)


def roll_lon(stacked, direction):
    rim_width = WB // 2
    extent = stacked.shape[3]
    outgoing = (
        stacked[:, :, :, :rim_width] if direction < 0 else stacked[:, :, :, extent - rim_width :]
    )
    incoming = from_behind(outgoing, "lon", direction)
    if direction < 0:
        return jnp.concatenate([stacked[:, :, :, rim_width:], incoming], axis=3)
    return jnp.concatenate([incoming, stacked[:, :, :, : extent - rim_width]], axis=3)


def roll_grid(stacked, direction):
    stacked = roll_lat(stacked, direction)
    stacked = roll_lon(stacked, direction)
    return jnp.roll(stacked, direction * (WL // 2), axis=1)


def shards(tokens, w_qkv, w_proj, bias_table, bias_index, regions, out_grad):
    both_inputs = jnp.stack([tokens, out_grad])
    rolled = roll_grid(both_inputs, -1)
    gathered = lax.all_gather(rolled, "tp", axis=4, tiled=True)
    normed, inv_std, normed_bf, grad_qkv, grad_flat, attended_flat = attention_grads(
        gathered[0], gathered[1], regions, w_qkv, w_proj, bias_table, bias_index
    )
    model_width = normed.shape[1]
    share_width = tokens.shape[3]
    inner_width = w_qkv.shape[2]
    offset = lax.axis_index("tp") * share_width
    part_value = jnp.dot(
        grad_qkv, w_qkv.reshape(model_width, 3 * inner_width).T, preferred_element_type=jnp.float32
    ).astype(jnp.bfloat16)
    part_input = lax.optimization_barrier(part_value).astype(jnp.float32)
    own_normed = lax.dynamic_slice_in_dim(normed, offset, share_width, 1)
    summed = lax.psum(part_input.astype(jnp.bfloat16), "tp").astype(jnp.float32)
    mean_grad = jnp.mean(summed, axis=1, keepdims=True)
    mean_cross = jnp.mean(summed * normed, axis=1, keepdims=True)
    own_grad = lax.dynamic_slice_in_dim(summed, offset, share_width, 1)
    grad_shifted = (inv_std * (own_grad - mean_grad - own_normed * mean_cross)).astype(jnp.bfloat16)
    grad_shifted = grad_shifted.reshape(tokens.shape)
    grad_tokens = roll_grid(grad_shifted[None], 1)[0]
    contract = (((0,), (0,)), ((), ()))
    qkv_part = lax.dot_general(normed_bf, grad_qkv, contract, preferred_element_type=jnp.float32)
    proj_part = lax.dot_general(
        grad_flat, attended_flat, contract, preferred_element_type=jnp.float32
    )
    summed_terms = lax.psum_scatter(
        jnp.concatenate([qkv_part, proj_part], axis=1),
        ("lat", "lon"),
        scatter_dimension=0,
        tiled=True,
    )
    qkv_grad = summed_terms[:, : 3 * inner_width].reshape(-1, 3, inner_width)
    proj_grad = summed_terms[:, 3 * inner_width :]
    return (grad_tokens, qkv_grad, proj_grad)


def solution(mesh):
    in_specs = (
        P(None, "lat", "lon", "tp"),
        P(None, None, "tp"),
        P(None, "tp"),
        P(None, "tp"),
        P(),
        P(None, "lat", "lon"),
        P(None, "lat", "lon", "tp"),
    )
    out_specs = (
        P(None, "lat", "lon", "tp"),
        P(("lat", "lon"), None, "tp"),
        P(("lat", "lon"), "tp"),
    )
    return jax.shard_map(shards, mesh=mesh, in_specs=in_specs, out_specs=out_specs, check_vma=False)
```

profile of v0, /device:TPU:0, one launch (start us, length us, event | category | flops | bytes accessed | tf_op | source)
XLA Modules:
  0.0 573.5 jit_solution(17154585913093884648)
XLA Ops:
  7.2 1.4 fusion.35
  8.6 4.3 collective-permute-start
  12.9 12.6 %collective-permute-done = bf16[2,4,3,24,512]{4,3,2,1,0:T(8,128)(2,1)S(1)} collective-permute-done((bf16[2,4,3,24,512]{4,3,2,1,0:T(8,128)(2,1)S(1)}, bf16[2,4,3,24,512]{4,3,2,1,0:T(8,128)(2,1)S(1)}, u32[]{:S(2)}, u32[]{:S(2)}) %collective-permute-start) | collective-permute-done | bytes 589856 | tf_op jit(solution)/shard_map/ppermute | solution.py:14
  25.5 1.6 collective-permute-start.1
  27.1 0.3 slice_maximum_fusion
  27.4 5.0 collective-permute-done.1
  32.4 0.2 fusion.34
  32.6 1.2 fusion.29
  33.9 0.2 copy.25
  34.1 0.1 reshape.103
  34.2 38.9 %gather_fusion = f32[20736,8]{1,0:T(8,128)} fusion(f32[759,8]{1,0:T(8,128)S(1)} %copy.25, s32[21504]{0:T(1024)S(1)} %pad_clamp_fusion), kind=kCustom, calls=%fused_computation | custom fusion | bytes 1410048 | tf_op jit(solution)/shard_map/jit(_take)/gather | solution.py:50
  73.1 11.2 %copy.26 = f32[144,144,8]{0,1,2:T(8,128)S(1)} copy(f32[144,144,8]{2,1,0:T(8,128)} %bitcast.86) | data formatting | bytes 1327104 | tf_op jit(solution)/shard_map/jit(_take)/gather | solution.py:50
  84.4 0.1 copy.24
  84.7 4.7 copy.21
  89.4 0.8 broadcast_compare_fusion
  90.2 1.1 select_bitcast_fusion
  91.4 1.6 convert_reduce_fusion
  93.0 1.7 multiply_reduce_fusion.2
  94.9 1.0 copy-done.7
  95.9 1.6 convolution_convert_fusion.4
  97.5 1.2 reshape_reshape.26
  98.7 1.4 copy.27
  100.1 3.2 reshape_reshape.27
  103.3 2.1 copy.28
  105.4 0.3 multiply_convert_fusion.1
  105.7 1.0 copy-done.8
  106.8 5.1 convolution_convert_fusion
  111.9 3.7 reshape_reshape.24
  115.6 4.7 copy.22
  120.3 6.8 %reshape_reshape.25 = bf16[4,144,3,8,64]{4,3,2,0,1:T(8,128)(2,1)} reshape(bf16[2,1,2,2,6,12,1536]{6,2,0,5,4,3,1:T(2,128)(2,1)} %copy.22) | data formatting | bytes 3538944 | tf_op jit(solution)/shard_map/reshape;reshape | solution.py:48
  127.1 15.0 %copy.23 = bf16[4,144,3,8,64]{1,4,3,0,2:T(8,128)(2,1)} copy(bf16[4,144,3,8,64]{4,3,2,0,1:T(8,128)(2,1)} %reshape_reshape.25) | data formatting | bytes 3538944 | tf_op jit(solution)/shard_map/reshape;reshape | solution.py:48
  142.2 4.4 fusion.33
  146.6 1.6 fusion.3
  148.2 2.1 copy-done.18
  150.3 2.5 fusion.27
  152.8 12.0 %fusion.21 = bf16[4,8,1,144,64]{3,4,1,0,2:T(8,128)(2,1)} fusion(f32[4,8,144,144]{2,3,1,0:T(8,128)} %fusion.33, bf16[3,4,8,144,64]{3,4,2,1,0:T(8,128)(2,1)} %bitcast.90, f32[4,8,144,144]{2,3,1,0:T(8,128)} %copy-done.18, f32[4,8,144]{2,1,0:T(8,128)S(1)} %get-tuple-element.15, f32[8,144,144]{1,2,0:T(8,128)} %select_bitcast_fusion, ...), kind=kOutput, calls=%fused_computation.26 | convolution fusion | flops 93860496 | bytes 23232512 | tf_op jit(solution)/shard_map/whij,whid->whjd/dot_general | solution.py:85
  164.9 12.0 %fusion.24 = bf16[4,8,1,144,64]{3,4,1,0,2:T(8,128)(2,1)} fusion(f32[4,8,144,144]{2,3,1,0:T(8,128)} %fusion.33, bf16[3,4,8,144,64]{3,4,2,1,0:T(8,128)(2,1)} %bitcast.91, f32[4,8,144,144]{2,3,1,0:T(8,128)} %copy-done.18, f32[4,8,144]{2,1,0:T(8,128)S(1)} %get-tuple-element.15, f32[8,144,144]{1,2,0:T(8,128)} %select_bitcast_fusion, ...), kind=kOutput, calls=%fused_computation.27 | convolution fusion | flops 93860496 | bytes 23232512 | tf_op jit(solution)/shard_map/whij,whjd->whid/dot_general | solution.py:82
  176.9 4.6 fusion.28
  181.5 2.6 maximum_bitcast_fusion
  184.1 6.6 %copy.33 = bf16[4,144,3,8,64]{4,3,2,0,1:T(8,128)(2,1)} copy(bf16[4,144,3,8,64]{1,4,3,0,2:T(8,128)(2,1)} %maximum_bitcast_fusion) | data formatting | bytes 3538944 | tf_op jit(solution)/shard_map/transpose | solution.py:89
  190.7 6.7 %reshape_reshape.28 = bf16[2,1,2,2,6,12,1536]{6,2,0,5,4,3,1:T(2,128)(2,1)} reshape(bf16[4,144,3,8,64]{4,3,2,0,1:T(8,128)(2,1)} %copy.33) | data formatting | bytes 3538944 | tf_op jit(solution)/shard_map/reshape;reshape | solution.py:26
  197.5 3.4 copy.34
  200.8 3.7 reshape_reshape.29
  204.6 5.5 convolution_convert_fusion.1
  210.1 1.9 copy.36
  212.0 3.0 reshape_reshape.30
  215.0 1.2 copy.37
  216.2 0.9 reshape_reshape.31
  217.2 3.9 fusion.50
  221.1 2.7 fusion.49
  223.8 5.7 pad_maximum_fusion
  229.7 1.8 fusion.12
  231.5 32.4 %all-reduce.2.cloned.1.call-done = bf16[576,1024]{1,0:T(8,128)(2,1)} async-done(((bf16[576,1024]{1,0:T(8,128)(2,1)}), bf16[576,1024]{1,0:T(8,128)(2,1)}) %all-reduce.2.cloned.1.call-update) | async-done | bytes 1179664 | tf_op jit(solution)/shard_map/psum | solution.py:140
  263.9 1.6 convert_element_type.69
  265.5 0.5 convert_reduce_fusion.1
  266.1 0.3 multiply_convert_fusion.2
  266.5 0.7 collective-permute-start.2
  267.2 10.2 %collective-permute-done.2 = bf16[1,4,3,24,512]{4,3,2,1,0:T(8,128)(2,1)S(1)} collective-permute-done((bf16[1,4,3,24,512]{4,3,2,1,0:T(8,128)(2,1)S(1)}, bf16[1,4,3,24,512]{4,3,2,1,0:T(8,128)(2,1)S(1)}, u32[]{:S(2)}, u32[]{:S(2)}) %collective-permute-start.2) | collective-permute-done | bytes 294944 | tf_op jit(solution)/shard_map/ppermute | solution.py:14
  277.5 6.3 %collective-permute-done.3 = bf16[1,4,6,6,512]{4,3,2,1,0:T(8,128)(2,1)S(1)} collective-permute-done((bf16[1,4,6,6,512]{4,3,2,1,0:T(8,128)(2,1)S(1)}, bf16[1,4,6,6,512]{4,3,2,1,0:T(8,128)(2,1)S(1)}, u32[]{:S(2)}, u32[]{:S(2)}) %collective-permute-start.3) | collective-permute-done | bytes 147488 | tf_op jit(solution)/shard_map/ppermute | solution.py:14
  283.8 1.0 fusion.37
  284.8 278.8 %reduce-scatter.2.cloned.1.call-done = f32[16,2048]{1,0:T(8,128)} async-done(((f32[1024,2048]{1,0:T(8,128)}), f32[16,2048]{1,0:T(8,128)}) %reduce-scatter.2.cloned.1.call-update) | async-done | bytes 131088 | tf_op jit(solution)/shard_map/reduce_scatter | solution.py:152
  563.7 0.9 slice.95
  564.6 0.6 copy.48
  565.2 1.4 slice.96
  (58 shorter events, 0.9 us)
Async XLA Ops:
  7.2 88.7 %copy-start = (bf16[1024,512]{1,0:T(8,128)(2,1)S(1)}, bf16[1024,512]{1,0:T(8,128)(2,1)}, u32[]{:S(2)}) copy-start(bf16[1024,512]{1,0:T(8,128)(2,1)} %param.9) | copy-start | bytes 3145732
  7.2 84.2 %all-gather.2.cloned.1.call-start = ((), (), s32[]{:S(2)}) async-start(), calls=%async_computation.1 | async-start | bytes 3538944 | tf_op jit(solution)/shard_map/all_gather | solution.py:127
  8.6 16.9 %collective-permute-start = (bf16[2,4,3,24,512]{4,3,2,1,0:T(8,128)(2,1)S(1)}, bf16[2,4,3,24,512]{4,3,2,1,0:T(8,128)(2,1)S(1)}, u32[]{:S(2)}, u32[]{:S(2)}) collective-permute-start(bf16[2,4,3,24,512]{4,3,2,1,0:T(8,128)(2,1)S(1)} %get-tuple-element.12), channel_id=1, source_target_pairs={{0,112},{16,0},{32,16},{48,32},{64,48},{80,64},{96,80},{112,96},{1... | collective-permute-start | bytes 1769480 | tf_op jit(solution)/shard_map/ppermute | solution.py:14
  25.5 6.9 %collective-permute-start.1 = (bf16[2,4,6,6,512]{4,3,2,1,0:T(8,128)(2,1)S(1)}, bf16[2,4,6,6,512]{4,3,2,1,0:T(8,128)(2,1)S(1)}, u32[]{:S(2)}, u32[]{:S(2)}) collective-permute-start(bf16[2,4,6,6,512]{4,3,2,1,0:T(8,128)(2,1)S(1)} %pad_maximum_fusion.7), channel_id=1, source_target_pairs={{0,14},{2,0},{4,2},{6,4},{8,6},{10,8},{12,10},{14,12},{1,15},{3,1}... | collective-permute-start | bytes 884744 | tf_op jit(solution)/shard_map/ppermute | solution.py:14
  32.6 1.3 copy-start.16
  32.6 1.4 copy-start.14
  33.8 230.1 %all-reduce.2.cloned.1.call-start = ((), (), s32[]{:S(2)}) async-start(), calls=%async_computation.2 | async-start | bytes 2359296 | tf_op jit(solution)/shard_map/psum | solution.py:140
  73.1 11.4 %copy-start.17 = (s32[4,6,24]{2,0,1:T(4,128)S(1)}, s32[4,6,24]{2,0,1:T(4,128)}, u32[]{:S(2)}) copy-start(s32[4,6,24]{2,0,1:T(4,128)} %param.12) | copy-start | bytes 6916
  91.4 3.4 copy-start.2
  94.9 1.0 copy-start.7
  105.7 1.1 copy-start.8
  142.1 4.4 copy-start.4
  142.1 4.4 copy-start.10
  142.1 4.4 copy-start.15
  148.2 2.1 copy-start.18
  176.9 4.6 copy-start.11
  176.9 4.6 copy-start.12
  176.9 4.6 copy-start.13
  210.1 353.6 %reduce-scatter.2.cloned.1.call-start = ((), (), s32[]{:S(2)}) async-start(), calls=%async_computation.3 | async-start | bytes 8519680 | tf_op jit(solution)/shard_map/reduce_scatter | solution.py:152
  217.2 3.9 copy-start.6
  217.2 4.0 copy-start.9
  231.5 34.0 %copy-start.3 = (f32[576,1024]{1,0:T(8,128)S(1)}, f32[576,1024]{1,0:T(8,128)}, u32[]{:S(2)}) copy-start(f32[576,1024]{1,0:T(8,128)} %fusion.12) | copy-start | bytes 7077892
  263.9 1.7 copy-start.5
  266.1 300.5 %copy-start.1 = (bf16[1024,512]{1,0:T(8,128)(2,1)S(1)}, bf16[1024,512]{1,0:T(8,128)(2,1)}, u32[]{:S(2)}) copy-start(bf16[1024,512]{1,0:T(8,128)(2,1)} %param.9) | copy-start | bytes 3145732
  266.5 10.9 %collective-permute-start.2 = (bf16[1,4,3,24,512]{4,3,2,1,0:T(8,128)(2,1)S(1)}, bf16[1,4,3,24,512]{4,3,2,1,0:T(8,128)(2,1)S(1)}, u32[]{:S(2)}, u32[]{:S(2)}) collective-permute-start(bf16[1,4,3,24,512]{4,3,2,1,0:T(8,128)(2,1)S(1)} %get-tuple-element.13), channel_id=1, source_target_pairs={{0,16},{16,32},{32,48},{48,64},{64,80},{80,96},{96,112},{112,0},{1... | collective-permute-start | bytes 884744 | tf_op jit(solution)/shard_map/ppermute | solution.py:14
  277.4 6.4 %collective-permute-start.3 = (bf16[1,4,6,6,512]{4,3,2,1,0:T(8,128)(2,1)S(1)}, bf16[1,4,6,6,512]{4,3,2,1,0:T(8,128)(2,1)S(1)}, u32[]{:S(2)}, u32[]{:S(2)}) collective-permute-start(bf16[1,4,6,6,512]{4,3,2,1,0:T(8,128)(2,1)S(1)} %pad_maximum_fusion.8), channel_id=1, source_target_pairs={{0,2},{2,4},{4,6},{6,8},{8,10},{10,12},{12,14},{14,0},{1,3},{3,5},... | collective-permute-start | bytes 442376 | tf_op jit(solution)/shard_map/ppermute | solution.py:14
Sparse Core Ops, SparseCore 0:
  33.9 42.8 all-gather.1
  210.2 53.6 all-reduce.1
  266.4 297.2 reduce-scatter.1
where the time goes:
time: 585 us; the launch traced here: 573 us
  waiting for transfers between devices  345 us (59%)
  local copies, waits for them, and re-layouts  128 us (22%)
  matrix products  56 us (10%)
  other arithmetic  22.5 us (4%)
  between operations  14.5 us (2%)
  starting transfers between devices  6.72 us (1%)
    reduce_scatter x1, waiting for transfers between devices, shards(): lax.psum_scatter(jnp.concatenate([qkv_part, proj_part], axis=1), ('lat',...  279 us
    gather x2, local copies, waits for them, and re-layouts, attention_grads(): table_bias = jnp.take(bias_table, bias_index, axis=0).transpose(2, 0, 1)  50.1 us
    ppermute x4, waiting for transfers between devices, from_behind(): lax.ppermute(value, axis, [(i, (i + by) % devices) for i in range(devices)])  34.1 us
    psum x1, waiting for transfers between devices, shards(): summed = lax.psum(part_input.astype(jnp.bfloat16), 'tp').astype(jnp.float32)  32.4 us
    another operation x2, local copies, waits for them, and re-layouts, attention_grads(): qkv_win.reshape(count_win, window, 3, head_count, HD)  21.8 us
    dot_general x1, matrix products, attention_grads(): jnp.einsum('whij,whjd->whid', grad_scores, key_part, preferred_element_ty...  12 us
    dot_general x1, matrix products, attention_grads(): jnp.einsum('whij,whid->whjd', grad_scores, queries, preferred_element_typ...  12 us
  transfers between devices with their start and end apart: 7, of which 6 were waited for; matrix products, arithmetic and copies ran while one was open for 14% of the time, Pallas kernels for 0%

commit v1 on v0

v1 whole, which is shorter than its diff:
```python
import functools

import jax
import jax.numpy as jnp
import numpy as np
from jax import lax
from jax.experimental import pallas as pl
from jax.experimental.pallas import tpu as pltpu
from jax.sharding import PartitionSpec as P

HD = 64
WT = 144
BIG = 112
SMALL = 48
PIECE = BIG + SMALL
MESH = pl.DeviceIdType.MESH
BF = jnp.bfloat16
F32 = jnp.float32
FAR = -1e30


def permutations():
    pack = np.zeros((2, PIECE, 288), np.float32)
    place = np.zeros((288, 2 * PIECE), np.float32)
    for di in range(2):
        for lv in range(2):
            for row in range(3):
                local = row + (3 if di == 0 else 0)
                for col in range(24):
                    if col >= 6:
                        spot = lv * 54 + row * 18 + col - 6
                    else:
                        spot = BIG + lv * 18 + row * 6 + col
                    pack[di, spot, lv * 144 + local * 24 + col] = 1
                    shifted = (col - 6) % 24
                    cell = (shifted // 12) * 144 + lv * 72 + (row + 3 * di) * 12 + shifted % 12
                    place[cell, di * PIECE + spot] = 1
    return pack, place


PACK, PLACE = permutations()


def position():
    lat, lon, tp = lax.axis_index("lat"), lax.axis_index("lon"), lax.axis_index("tp")
    return lat, lon, tp


def device(lat, lon, tp):
    return {"lat": lat, "lon": lon, "tp": tp}


def neighbours():
    lat, lon, tp = position()
    x, zl, y, core = lat // 2, lat % 2, lon // 2, lon % 2
    sibling = device(lat, y * 2 + 1 - core, tp)
    along_x = [device(((x + d) % 4) * 2 + zl, lon, tp) for d in (1, 2, 3)]
    along_y = [device(lat, ((y + d) % 4) * 2 + core, tp) for d in (1, 2, 3)]
    along_z = device(x * 2 + 1 - zl, lon, tp)
    partner = device(lat, lon, 1 - tp)
    return x, zl, y, core, sibling, along_x, along_y, along_z, partner


def enter(targets):
    barrier = pltpu.get_barrier_semaphore()
    for target in targets:
        pl.semaphore_signal(barrier, inc=1, device_id=target, device_id_type=MESH)
    pl.semaphore_wait(barrier, len(targets))


def piece_ends(sign):
    lat, lon, tp = position()
    ends = []
    for di in range(2):
        for dj in range(2):
            for other in range(2):
                if di == 0 and dj == 0 and other == 0:
                    continue
                to_tp = 1 - tp if other else tp
                ends.append((di, dj, to_tp, device((lat + sign * di + 8) % 8, (lon + sign * dj + 8) % 8, to_tp)))
    return ends


def send(src, dst, send_sem, recv_sem, target):
    copy = pltpu.make_async_remote_copy(
        src_ref=src, dst_ref=dst, send_sem=send_sem, recv_sem=recv_sem, device_id=target, device_id_type=MESH
    )
    copy.start()
    return copy


def bring_kernel(tok_ref, grad_ref, pack_ref, wq_ref, wp_ref, table_ref, held_ref, other_ref, tables_ref,
                 packed, piece_send, piece_recv, w_send, w_recv, local_sem):
    lat, lon, tp = position()
    x, zl, y, core, sibling, along_x, along_y, along_z, partner = neighbours()
    ends = piece_ends(-1)
    sources = piece_ends(1)
    enter([e[3] for e in sources] + [sibling, along_z, partner] + along_x + along_y)

    mine = ((x * 2 + zl) * 4 + y) * 2 + core
    first = [
        send(wq_ref.at[:, mine], other_ref.at[0:3, x, zl, y, core], w_send.at[0], w_recv.at[0], partner),
        send(wp_ref.at[mine], other_ref.at[3, x, zl, y, core], w_send.at[1], w_recv.at[1], partner),
    ]
    tables_ref[0] = jnp.zeros((8, 768), F32)
    tables_ref[0, :, 0:759] = table_ref[...]
    table_copy = send(tables_ref.at[0], tables_ref.at[1], w_send.at[2], w_recv.at[2], partner)

    for half in range(2):
        for di in range(2):
            for which, ref in enumerate((tok_ref, grad_ref)):
                if half == 0:
                    cells = ref[144:432, :]
                else:
                    cells = jnp.concatenate([ref[432:576, :], ref[0:144, :]], axis=0)
                moved = jnp.dot(pack_ref[di], cells, preferred_element_type=F32).astype(BF)
                packed[half, di, which * BIG:(which + 1) * BIG, :] = moved[0:BIG]
                base = 2 * BIG + which * SMALL
                packed[half, di, base:base + SMALL, :] = moved[BIG:PIECE]

    spans = (pl.ds(0, 2 * BIG), pl.ds(2 * BIG, 2 * SMALL))
    pieces = []
    for n, (di, dj, to_tp, target) in enumerate(ends):
        pieces.append(send(packed.at[to_tp, di, spans[dj]], held_ref.at[tp, di, spans[dj]],
                           piece_send.at[n], piece_recv.at[n], target))
    own = pltpu.make_async_copy(packed.at[tp, 0, spans[0]], held_ref.at[tp, 0, spans[0]], local_sem)
    own.start()

    for copy in first:
        copy.wait()
    second = send(other_ref.at[:, x, zl, y, core], other_ref.at[:, x, zl, y, core], w_send.at[3], w_recv.at[3], along_z)
    second.wait()
    third = []
    for d in range(3):
        third.append(send(other_ref.at[0:2, x, :, y, core], other_ref.at[0:2, x, :, y, core],
                          w_send.at[4 + d], w_recv.at[4 + d], along_x[d]))
        third.append(send(other_ref.at[2:4, x, :, y, core], other_ref.at[2:4, x, :, y, core],
                          w_send.at[7 + d], w_recv.at[7 + d], along_y[d]))
    for copy in third:
        copy.wait()
    fourth = []
    for d in range(3):
        fourth.append(send(other_ref.at[0:2, :, :, y, core], other_ref.at[0:2, :, :, y, core],
                           w_send.at[10 + d], w_recv.at[10 + d], along_y[d]))
        fourth.append(send(other_ref.at[2:4, x, :, :, core], other_ref.at[2:4, x, :, :, core],
                           w_send.at[13 + d], w_recv.at[13 + d], along_x[d]))
    for copy in fourth:
        copy.wait()
    fifth = send(other_ref.at[:, :, :, :, core], other_ref.at[:, :, :, :, core], w_send.at[16], w_recv.at[16], sibling)
    fifth.wait()
    own.wait()
    table_copy.wait()
    for copy in pieces:
        copy.wait()


def bias_kernel(tables_ref, index_ref, regions_ref, bias_ref):
    tp = lax.axis_index("tp")
    rows = lax.broadcasted_iota(jnp.int32, (WT, WT), 0) // 12
    cols = lax.broadcasted_iota(jnp.int32, (WT, WT), 1) // 12
    left = jnp.zeros((WT, WT), jnp.int32)
    right = jnp.zeros((WT, WT), jnp.int32)
    for lv in range(2):
        for row in range(6):
            value = regions_ref[2 * tp + lv, row, 0]
            left = jnp.where(rows == lv * 6 + row, value, left)
            right = jnp.where(cols == lv * 6 + row, value, right)
    blocked = jnp.where(left == right, 0.0, FAR).astype(F32)

    blocks = []
    for s in range(2):
        table = tables_ref[s]
        top = table.astype(BF).astype(F32)
        rest = table - top
        mid = rest.astype(BF).astype(F32)
        low = rest - mid
        for part in (top, mid, low):
            for g in range(3):
                blocks.append(part[:, g * 256:(g + 1) * 256])
    matrix = jnp.concatenate(blocks, axis=0).astype(BF)
    depth = lax.broadcasted_iota(jnp.int32, (256, WT), 0)

    def some_rows(step, carry):
        found = ([], [])
        index = index_ref[pl.ds(pl.multiple_of(step * 8, 8), 8), :]
        for r in range(8):
            row = index[r:r + 1, :]
            low_part, high_part = row & 255, row >> 8
            hot = jnp.where(depth == low_part, 1.0, 0.0).astype(BF)
            picked = jnp.dot(matrix, hot, preferred_element_type=F32)
            for s in range(2):
                total = jnp.zeros((8, WT), F32)
                for g in range(3):
                    base = s * 72 + g * 8
                    value = picked[base:base + 8] + picked[base + 24:base + 32] + picked[base + 48:base + 56]
                    total = jnp.where(high_part == g, value, total)
                found[s].append(total)
        for s in range(2):
            stacked = jnp.stack(found[s], axis=0)
            bias_ref[s * 8:(s + 1) * 8, pl.ds(pl.multiple_of(step * 8, 8), 8), :] = jnp.transpose(stacked, (1, 0, 2))
        return carry

    lax.fori_loop(0, WT // 8, some_rows, 0)
    for h in range(16):
        bias_ref[h] = bias_ref[h] + blocked


def work_kernel(held_ref, place_ref, placet_ref, wq_ref, wp_ref, other_ref, bias_ref, sums_ref, back_ref,
                normed, normed_bf, grads, normed_t, grads_t, inv, parts, dparts, att, dx):
    def gather(which):
        halves = []
        for t in range(2):
            rows = []
            for di in range(2):
                rows.append(held_ref[t, di, which * BIG:(which + 1) * BIG, :])
                base = 2 * BIG + which * SMALL
                rows.append(held_ref[t, di, base:base + SMALL, :])
            halves.append(jnp.dot(place_ref[...], jnp.concatenate(rows, axis=0), preferred_element_type=F32))
        return jnp.concatenate(halves, axis=1)

    cells = gather(0)
    center = jnp.mean(cells, axis=1, keepdims=True)
    cells = cells - center
    spread = jnp.mean(jnp.square(cells), axis=1, keepdims=True)
    inv_std = lax.rsqrt(spread + 1e-05)
    cells = cells * inv_std
    normed[...] = cells
    normed_bf[...] = cells.astype(BF)
    inv[...] = jnp.broadcast_to(inv_std, (288, 128))
    normed_t[...] = jnp.transpose(normed_bf[...], (1, 0))
    grads[...] = gather(1).astype(BF)
    grads_t[...] = jnp.transpose(grads[...], (1, 0))

    lane = lax.broadcasted_iota(jnp.int32, (WT, 128), 1)
    first = lane < HD

    def split(value):
        zero = jnp.zeros_like(value)
        return jnp.concatenate([jnp.where(first, value, zero), jnp.where(first, zero, value)], axis=0)

    for half in range(2):
        def weight(c):
            if half == 0:
                return wq_ref.at[c] if c < 3 else wp_ref
            return other_ref.at[c]

        for c in range(4):
            left = normed_bf if c < 3 else grads
            value = jnp.dot(left[...], weight(c)[...], preferred_element_type=F32)
            value = value.astype(BF)
            if c == 0:
                value = value * jnp.asarray(0.125, BF)
            parts[c] = value

        def pair(p, carry):
            span = pl.ds(pl.multiple_of(p * 128, 128), 128)
            for w in range(2):
                rows = pl.ds(w * WT, WT)
                q, k, v, g = (parts[c, rows, span] for c in range(4))
                qq, gg = split(q), split(g)
                bias = jnp.concatenate([bias_ref[half * 8 + 2 * p], bias_ref[half * 8 + 2 * p + 1]], axis=0)
                contract = (((1,), (1,)), ((), ()))
                flip = (((0,), (0,)), ((), ()))
                scores = lax.dot_general(qq, k, contract, preferred_element_type=F32) + bias
                weights = jnp.exp(scores)
                probs = weights / jnp.sum(weights, axis=1, keepdims=True)
                probs_bf = probs.astype(BF)
                found = jnp.dot(probs_bf, v, preferred_element_type=F32)
                att[rows, span] = jnp.where(first, found[0:WT], found[WT:]).astype(BF)
                gprobs = lax.dot_general(gg, v, contract, preferred_element_type=F32)
                dot_sum = jnp.sum(probs * gprobs, axis=1, keepdims=True)
                gscores = (probs * (gprobs - dot_sum)).astype(BF)
                gq = jnp.dot(gscores, k, preferred_element_type=F32)
                dparts[0, rows, span] = (jnp.where(first, gq[0:WT], gq[WT:]) * 0.125).astype(BF)
                dparts[1, rows, span] = lax.dot_general(gscores, qq, flip, preferred_element_type=F32).astype(BF)
                dparts[2, rows, span] = lax.dot_general(probs_bf, gg, flip, preferred_element_type=F32).astype(BF)
            return carry

        lax.fori_loop(0, 4, pair, 0)

        for c in range(3):
            value = lax.dot_general(dparts[c], weight(c)[...], (((1,), (1,)), ((), ())), preferred_element_type=F32)
            if half == 0 and c == 0:
                dx[...] = value
            else:
                dx[...] += value

        for c in range(4):
            left = normed_t if c < 3 else grads_t

            def block(r, carry):
                rows = pl.ds(pl.multiple_of(r * 256, 256), 256)
                right = dparts[c] if c < 3 else att[...]
                sums_ref[2 * c + half, rows, :] = jnp.dot(left[rows, :], right, preferred_element_type=F32).astype(BF)
                return carry

            lax.fori_loop(0, 4, block, 0)

    total = dx[...]
    mean_grad = jnp.mean(total, axis=1, keepdims=True)
    mean_cross = jnp.mean(total * normed[...], axis=1, keepdims=True)
    result = (inv[:, 0:1] * (total - mean_grad - normed[...] * mean_cross)).astype(BF)
    moved = jnp.dot(placet_ref[...], result, preferred_element_type=F32).astype(BF)
    for di in range(2):
        for t in range(2):
            back_ref[t, di] = moved[di * PIECE:(di + 1) * PIECE, t * 512:(t + 1) * 512]


def take_kernel(sums_ref, back_ref, packt_ref, tokens_ref, total_ref,
                landed, core_in, core_sum, xa_in, yb_in, xa_sum, yb_sum, ya_in, xb_in, z_out, z_in, t_out, t_in,
                piece_send, piece_recv, r_send, r_recv, local_sem):
    lat, lon, tp = position()
    x, zl, y, core, sibling, along_x, along_y, along_z, partner = neighbours()
    ends = piece_ends(1)
    sources = piece_ends(-1)
    enter([e[3] for e in sources] + [sibling, along_z, partner] + along_x + along_y)

    core_copy = send(sums_ref.at[:, :, 1 - core], core_in, r_send.at[0], r_recv.at[0], sibling)
    spans = (pl.ds(0, BIG), pl.ds(BIG, SMALL))
    pieces = []
    for n, (di, dj, to_tp, target) in enumerate(ends):
        pieces.append(send(back_ref.at[to_tp, di, spans[dj]], landed.at[tp, di, spans[dj]],
                           piece_send.at[n], piece_recv.at[n], target))
    own = pltpu.make_async_copy(back_ref.at[tp, 0, spans[0]], landed.at[tp, 0, spans[0]], local_sem)
    own.start()

    core_copy.wait()

    def add_core(n, carry):
        for k in range(4):
            rows = pl.ds(k * 8, 8)
            value = sums_ref[n, rows, core].astype(F32) + core_in[n, rows].astype(F32)
            core_sum[n, k] = value.reshape(2, 4, 16, 512).astype(BF)
        return carry

    lax.fori_loop(0, 8, add_core, 0)

    stage = []
    for d in range(3):
        stage.append(send(core_sum.at[0:4, (x + d + 1) % 4], xa_in.at[d], r_send.at[1 + d], r_recv.at[1 + d], along_x[d]))
        stage.append(send(core_sum.at[4:8, :, :, (y + d + 1) % 4], yb_in.at[d], r_send.at[4 + d], r_recv.at[4 + d], along_y[d]))
    for copy in stage:
        copy.wait()

    def add_first(n, carry):
        value = core_sum[n, x].astype(F32)
        for d in range(3):
            value += xa_in[d, n].astype(F32)
        xa_sum[n] = value.astype(BF)
        value = core_sum[4 + n, :, :, y].astype(F32)
        for d in range(3):
            value += yb_in[d, n].astype(F32)
        yb_sum[n] = value.astype(BF)
        return carry

    lax.fori_loop(0, 4, add_first, 0)

    stage = []
    for d in range(3):
        stage.append(send(xa_sum.at[:, :, (y + d + 1) % 4], ya_in.at[d], r_send.at[7 + d], r_recv.at[7 + d], along_y[d]))
        stage.append(send(yb_sum.at[:, (x + d + 1) % 4], xb_in.at[d], r_send.at[10 + d], r_recv.at[10 + d], along_x[d]))
    for copy in stage:
        copy.wait()

    def add_second(n, carry):
        value = xa_sum[n, :, y].astype(F32)
        for d in range(3):
            value += ya_in[d, n].astype(F32)
        z_out[n] = value.astype(BF)
        value = yb_sum[n, x].astype(F32)
        for d in range(3):
            value += xb_in[d, n].astype(F32)
        z_out[4 + n] = value.astype(BF)
        return carry

    lax.fori_loop(0, 4, add_second, 0)

    z_copy = send(z_out.at[:, 1 - zl], z_in, r_send.at[13], r_recv.at[13], along_z)
    z_copy.wait()
    for c in range(4):
        t_out[c] = (z_out[2 * c + 1, zl].astype(F32) + z_in[2 * c + 1].astype(F32)).astype(BF)
    t_copy = send(t_out, t_in, r_send.at[14], r_recv.at[14], partner)

    own.wait()
    for copy in pieces:
        copy.wait()
    for t in range(2):
        cells = landed[t].reshape(2 * PIECE, 512)
        moved = jnp.dot(packt_ref[...], cells, preferred_element_type=F32).astype(BF)
        if t == 0:
            tokens_ref[144:432, :] = moved
        else:
            tokens_ref[432:576, :] = moved[0:144]
            tokens_ref[0:144, :] = moved[144:288]

    t_copy.wait()
    for c in range(4):
        total_ref[c] = z_out[2 * c, zl].astype(F32) + z_in[2 * c].astype(F32) + t_in[c].astype(F32)


VM = pl.BlockSpec(memory_space=pltpu.VMEM)
SM = pl.BlockSpec(memory_space=pltpu.SMEM)
LIMIT = 56 * 1024 * 1024


def shards(tokens, w_qkv, w_proj, bias_table, bias_index, regions, out_grad):
    flat_in = tokens.reshape(576, 512)
    flat_grad = out_grad.reshape(576, 512)
    wq = w_qkv.transpose(1, 0, 2)
    pack = jnp.asarray(PACK, BF)
    packt = jnp.asarray(np.concatenate([PACK[0].T, PACK[1].T], axis=1), BF)
    place = jnp.asarray(PLACE, BF)
    placet = jnp.asarray(PLACE.T, BF)
    dma = pltpu.SemaphoreType.DMA
    shape = jax.ShapeDtypeStruct
    held, other, tables = pl.pallas_call(
        bring_kernel,
        out_shape=(
            shape((2, 2, 2 * PIECE, 512), BF),
            shape((4, 4, 2, 4, 2, 16, 512), BF),
            shape((2, 8, 768), F32),
        ),
        in_specs=[VM] * 6,
        out_specs=(VM, VM, VM),
        scratch_shapes=[
            pltpu.VMEM((2, 2, 2 * PIECE, 512), BF),
            dma((7,)), dma((7,)), dma((17,)), dma((17,)), dma,
        ],
        compiler_params=pltpu.CompilerParams(collective_id=0, has_side_effects=True, vmem_limit_bytes=LIMIT),
        name="bring",
    )(flat_in, flat_grad, pack, wq.reshape(3, 64, 16, 512), w_proj.reshape(64, 16, 512), bias_table.T)

    bias = pl.pallas_call(
        bias_kernel,
        out_shape=shape((16, WT, WT), F32),
        in_specs=[VM, VM, SM],
        out_specs=VM,
        compiler_params=pltpu.CompilerParams(vmem_limit_bytes=LIMIT),
        name="bias",
    )(tables, bias_index, regions)

    vmem = pltpu.VMEM
    sums, back = pl.pallas_call(
        work_kernel,
        out_shape=(shape((8, 1024, 512), BF), shape((2, 2, PIECE, 512), BF)),
        in_specs=[VM] * 7,
        out_specs=(VM, VM),
        scratch_shapes=[
            vmem((288, 1024), F32), vmem((288, 1024), BF), vmem((288, 1024), BF), vmem((1024, 288), BF),
            vmem((1024, 288), BF), vmem((288, 128), F32), vmem((4, 288, 512), BF), vmem((3, 288, 512), BF),
            vmem((288, 512), BF), vmem((288, 1024), F32),
        ],
        compiler_params=pltpu.CompilerParams(vmem_limit_bytes=LIMIT),
        name="work",
    )(held, place, placet, wq, w_proj, other.reshape(4, 1024, 512), bias)

    grad_tokens, total = pl.pallas_call(
        take_kernel,
        out_shape=(shape((576, 512), BF), shape((4, 16, 512), F32)),
        in_specs=[VM] * 3,
        out_specs=(VM, VM),
        scratch_shapes=[
            vmem((2, 2, PIECE, 512), BF),
            vmem((8, 32, 16, 512), BF), vmem((8, 4, 2, 4, 16, 512), BF),
            vmem((3, 4, 2, 4, 16, 512), BF), vmem((3, 4, 4, 2, 16, 512), BF),
            vmem((4, 2, 4, 16, 512), BF), vmem((4, 4, 2, 16, 512), BF),
            vmem((3, 4, 2, 16, 512), BF), vmem((3, 4, 2, 16, 512), BF),
            vmem((8, 2, 16, 512), BF), vmem((8, 16, 512), BF),
            vmem((4, 16, 512), BF), vmem((4, 16, 512), BF),
            dma((7,)), dma((7,)), dma((15,)), dma((15,)), dma,
        ],
        compiler_params=pltpu.CompilerParams(collective_id=1, has_side_effects=True, vmem_limit_bytes=LIMIT),
        name="take",
    )(sums.reshape(8, 32, 2, 16, 512), back, packt)

    qkv_grad = total[0:3].transpose(1, 0, 2)
    proj_grad = total[3]
    return grad_tokens.reshape(tokens.shape), qkv_grad, proj_grad


def solution(mesh):
    in_specs = (
        P(None, "lat", "lon", "tp"),
        P(None, None, "tp"),
        P(None, "tp"),
        P(None, "tp"),
        P(),
        P(None, "lat", "lon"),
        P(None, "lat", "lon", "tp"),
    )
    out_specs = (
        P(None, "lat", "lon", "tp"),
        P(("lat", "lon"), None, "tp"),
        P(("lat", "lon"), "tp"),
    )
    return jax.shard_map(shards, mesh=mesh, in_specs=in_specs, out_specs=out_specs, check_vma=False)
```

time: 585 us -> 165 us (0.28); the launches traced: 573 us -> 165 us
  waiting for transfers between devices: 345 us -> 0 us
  Pallas kernels: 0 us -> 158 us
  local copies, waits for them, and re-layouts: 128 us -> 6.15 us
  matrix products: 56 us -> 0 us
  other arithmetic: 22.5 us -> 0 us
  between operations: 14.5 us -> 0.65 us
  starting transfers between devices: 6.72 us -> 0 us
    reduce_scatter x1 -> x0, waiting for transfers between devices: 279 us -> none  [shards(): lax.psum_scatter(jnp.concatenate([qkv_part, proj_part], axis=1), ('lat',...]
    pallas_call x0 -> x4, Pallas kernels: none -> 158 us  [the longest x1 60.3 us: shards(): pl.pallas_call(take_kernel, out_shape=(shape((576, 512), BF), shape((4, 1...]
    dot_general x11 -> x0, matrix products: 56 us -> none  [the longest x1 12 us: attention_grads(): jnp.einsum('whij,whjd->whid', grad_scores, key_part, preferred_element_ty...]
    gather x2 -> x0, local copies, waits for them, and re-layouts: 50.1 us -> none  [attention_grads(): table_bias = jnp.take(bias_table, bias_index, axis=0).transpose(2, 0, 1)]
    another operation x11 -> x0, local copies, waits for them, and re-layouts: 44.4 us -> none  [the longest x2 21.8 us: attention_grads(): qkv_win.reshape(count_win, window, 3, head_count, HD)]
    ppermute x4 -> x0, waiting for transfers between devices: 34.1 us -> none  [from_behind(): lax.ppermute(value, axis, [(i, (i + by) % devices) for i in range(devices)])]
    psum x1 -> x0, waiting for transfers between devices: 32.4 us -> none  [shards(): summed = lax.psum(part_input.astype(jnp.bfloat16), 'tp').astype(jnp.float32)]
    transpose x6 -> x1, local copies, waits for them, and re-layouts: 19.4 us -> 1.54 us  [shards(): qkv_grad = total[0:3].transpose(1, 0, 2)]
  transfers between devices with their start and end apart: 7 -> 0, of which waited for: 6 -> 0; matrix products, arithmetic and copies ran while one was open for 14% -> 0% of each run, Pallas kernels for 0% -> 0%
where the time goes in v1:
time: 165 us
  Pallas kernels  158 us (96%)
  local copies, waits for them, and re-layouts  6.15 us (4%)
    pallas_call x1, Pallas kernels, shards(): pl.pallas_call(take_kernel, out_shape=(shape((576, 512), BF), shape((4, 1...  60.3 us
    pallas_call x1, Pallas kernels, shards(): pl.pallas_call(bring_kernel, out_shape=(shape((2, 2, 2 * PIECE, 512), BF)...  54.7 us
    pallas_call x1, Pallas kernels, shards(): pl.pallas_call(work_kernel, out_shape=(shape((8, 1024, 512), BF), shape((...  34 us
    pallas_call x1, Pallas kernels, shards(): pl.pallas_call(bias_kernel, out_shape=shape((16, WT, WT), F32), in_specs=...  9.01 us

profile of v1, /device:TPU:0, one launch (start us, length us, event | category | flops | bytes accessed | tf_op | source)
XLA Modules:
  0.0 164.8 jit_solution(9144777311270413554)
XLA Ops:
  0.6 1.3 copy.14.regions_ref
  1.9 54.7 %bring.1 = (bf16[2,2,320,512]{3,2,1,0:T(8,128)(2,1)}, bf16[4,4,2,4,2,16,512]{6,5,4,3,2,1,0:T(8,128)(2,1)}, f32[2,8,768]{2,1,0:T(8,128)}) custom-call(bf16[576,512]{1,0:T(8,128)(2,1)} %bitcast.20, bf16[576,512]{1,0:T(8,128)(2,1)} %bitcast.21, bf16[2,160,288]{2,1,0:T(8,128)(2,1)} %constant.8.clone.pack_ref, bf16[3,64,16,512]{3,2,1,0:T(8,128)(2,1)} %bitcast.14, ...), custom_call_target="tpu_custom_call" | custom-call | tf_op jit(solution)/shard_map/bring/pallas_call | solution.py:416
  56.6 9.0 %bias.1.bias_ref = f32[16,144,144]{2,1,0:T(8,128)} custom-call(f32[2,8,768]{2,1,0:T(8,128)} %get-tuple-element.12.tables_ref, s32[144,144]{1,0:T(8,128)} %index_ref.1, s32[4,6,24]{2,1,0:T(8,128)} %copy.14.regions_ref), custom_call_target="tpu_custom_call" | custom-call | tf_op jit(solution)/shard_map/bias/pallas_call | solution.py:433
  65.6 34.0 %work.1 = (bf16[8,1024,512]{2,1,0:T(8,128)(2,1)}, bf16[2,2,160,512]{3,2,1,0:T(8,128)(2,1)}) custom-call(bf16[2,2,320,512]{3,2,1,0:T(8,128)(2,1)} %get-tuple-element.10.held_ref, bf16[288,320]{1,0:T(8,128)(2,1)} %constant.10.clone.place_ref, bf16[320,288]{1,0:T(8,128)(2,1)} %constant.11.clone.placet_ref, bf16[3,1024,512]{2,1,0:T(8,128)(2,1)} %bitcast.15, ...), custom_call_target="tpu_custom_call" | custom-call | tf_op jit(solution)/shard_map/work/pallas_call | solution.py:443
  99.7 60.3 %take.1 = (bf16[576,512]{1,0:T(8,128)(2,1)}, f32[4,16,512]{2,1,0:T(8,128)}) custom-call(bf16[8,32,2,16,512]{4,3,2,1,0:T(8,128)(2,1)} %bitcast.16, bf16[2,2,160,512]{3,2,1,0:T(8,128)(2,1)} %get-tuple-element.14.back_ref, bf16[288,320]{1,0:T(8,128)(2,1)} %constant.9.clone.packt_ref), custom_call_target="tpu_custom_call" | custom-call | tf_op jit(solution)/shard_map/take/pallas_call | solution.py:457
  160.0 1.4 slice_bitcast_fusion.1
  161.3 1.5 slice_bitcast_fusion
  162.9 1.9 %copy.16 = bf16[4,6,24,512]{3,2,1,0:T(8,128)(2,1)} copy(bf16[4,6,24,512]{3,2,1,0:T(8,128)(2,1)} %bitcast.19) | data formatting | bytes 1179648

commit v2 on v1

v2 whole, which is shorter than its diff:
```python
import functools

import jax
import jax.numpy as jnp
import numpy as np
from jax import lax
from jax.experimental import pallas as pl
from jax.experimental.pallas import tpu as pltpu
from jax.sharding import PartitionSpec as P

HD = 64
WT = 144
BIG = 112
SMALL = 48
PIECE = BIG + SMALL
MESH = pl.DeviceIdType.MESH
BF = jnp.bfloat16
F32 = jnp.float32
FAR = -1e30


def permutations():
    pack = np.zeros((2, PIECE, 288), np.float32)
    place = np.zeros((288, 2 * PIECE), np.float32)
    for di in range(2):
        for lv in range(2):
            for row in range(3):
                local = row + (3 if di == 0 else 0)
                for col in range(24):
                    if col >= 6:
                        spot = lv * 54 + row * 18 + col - 6
                    else:
                        spot = BIG + lv * 18 + row * 6 + col
                    pack[di, spot, lv * 144 + local * 24 + col] = 1
                    shifted = (col - 6) % 24
                    cell = (shifted // 12) * 144 + lv * 72 + (row + 3 * di) * 12 + shifted % 12
                    place[cell, di * PIECE + spot] = 1
    return pack, place


PACK, PLACE = permutations()


def position():
    lat, lon, tp = lax.axis_index("lat"), lax.axis_index("lon"), lax.axis_index("tp")
    return lat, lon, tp


def device(lat, lon, tp):
    return {"lat": lat, "lon": lon, "tp": tp}


def neighbours():
    lat, lon, tp = position()
    x, zl, y, core = lat // 2, lat % 2, lon // 2, lon % 2
    sibling = device(lat, y * 2 + 1 - core, tp)
    along_x = [device(((x + d) % 4) * 2 + zl, lon, tp) for d in (1, 2, 3)]
    along_y = [device(lat, ((y + d) % 4) * 2 + core, tp) for d in (1, 2, 3)]
    along_z = device(x * 2 + 1 - zl, lon, tp)
    partner = device(lat, lon, 1 - tp)
    return x, zl, y, core, sibling, along_x, along_y, along_z, partner


def piece_ends(sign):
    lat, lon, tp = position()
    ends = []
    for di in range(2):
        for dj in range(2):
            for other in range(2):
                if di == 0 and dj == 0 and other == 0:
                    continue
                to_tp = 1 - tp if other else tp
                ends.append((di, dj, to_tp, device((lat + sign * di + 8) % 8, (lon + sign * dj + 8) % 8, to_tp)))
    return ends


def send(src, dst, send_sem, recv_sem, target):
    copy = pltpu.make_async_remote_copy(
        src_ref=src, dst_ref=dst, send_sem=send_sem, recv_sem=recv_sem, device_id=target, device_id_type=MESH
    )
    copy.start()
    return copy


def whole_kernel(tok_ref, grad_ref, pack_ref, place_ref, placet_ref, wq_hbm, wp_hbm, table_ref, index_ref, regions_ref,
                 landed, total_ref,
                 wq_ref, wp_ref, other_ref, tables_ref, packed, held, bias_ref,
                 normed, normed_bf, grads, normed_t, grads_t, inv, parts, dparts, att, dx, back,
                 sums, core_in, core_sum, xa_in, yb_in, xa_sum, yb_sum, ya_in, xb_in, z_out, z_in, t_out, t_in,
                 piece_send, piece_recv, back_send, back_recv, w_send, w_recv, r_send, r_recv, local_sem):
    lat, lon, tp = position()
    x, zl, y, core, sibling, along_x, along_y, along_z, partner = neighbours()
    ahead, behind = piece_ends(-1), piece_ends(1)
    barrier = pltpu.get_barrier_semaphore()
    targets = [e[3] for e in ahead] + [e[3] for e in behind] + [sibling, along_z, partner] + along_x + along_y
    for target in targets:
        pl.semaphore_signal(barrier, inc=1, device_id=target, device_id_type=MESH)

    own_weights = [
        pltpu.make_async_copy(wq_hbm, wq_ref, local_sem.at[0]),
        pltpu.make_async_copy(wp_hbm, wp_ref, local_sem.at[1]),
    ]
    for copy in own_weights:
        copy.start()

    tables_ref[0] = jnp.zeros((8, 768), F32)
    tables_ref[0, :, 0:759] = table_ref[...]

    def pack(half):
        for di in range(2):
            for which, ref in enumerate((tok_ref, grad_ref)):
                if half == 0:
                    cells = ref[144:432, :]
                else:
                    cells = jnp.concatenate([ref[432:576, :], ref[0:144, :]], axis=0)
                moved = jnp.dot(pack_ref[di], cells, preferred_element_type=F32).astype(BF)
                packed[half, di, which * BIG:(which + 1) * BIG, :] = moved[0:BIG]
                base = 2 * BIG + which * SMALL
                packed[half, di, base:base + SMALL, :] = moved[BIG:PIECE]

    pack(0)
    pack(1)
    pl.semaphore_wait(barrier, len(targets))

    mine = ((x * 2 + zl) * 4 + y) * 2 + core
    first = [
        send(wq_hbm.at[:, mine], other_ref.at[0:3, x, zl, y, core], w_send.at[0], w_recv.at[0], partner),
        send(wp_hbm.at[mine], other_ref.at[3, x, zl, y, core], w_send.at[1], w_recv.at[1], partner),
        send(tables_ref.at[0], tables_ref.at[1], w_send.at[2], w_recv.at[2], partner),
    ]
    spans = (pl.ds(0, 2 * BIG), pl.ds(2 * BIG, 2 * SMALL))
    pieces = []
    for n, (di, dj, to_tp, target) in enumerate(ahead):
        pieces.append(send(packed.at[to_tp, di, spans[dj]], held.at[tp, di, spans[dj]],
                           piece_send.at[n], piece_recv.at[n], target))
    own = pltpu.make_async_copy(packed.at[tp, 0, spans[0]], held.at[tp, 0, spans[0]], local_sem.at[2])
    own.start()
    pieces.append(own)

    rows = lax.broadcasted_iota(jnp.int32, (WT, WT), 0) // 12
    cols = lax.broadcasted_iota(jnp.int32, (WT, WT), 1) // 12
    left = jnp.zeros((WT, WT), jnp.int32)
    right = jnp.zeros((WT, WT), jnp.int32)
    for lv in range(2):
        for row in range(6):
            value = regions_ref[row, pl.ds(2 * tp + lv, 1), 0:1]
            left = jnp.where(rows == lv * 6 + row, value, left)
            right = jnp.where(cols == lv * 6 + row, value, right)
    blocked = jnp.where(left == right, 0.0, FAR).astype(F32)

    for copy in first:
        copy.wait()
    second = send(other_ref.at[:, x, zl, y, core], other_ref.at[:, x, zl, y, core], w_send.at[3], w_recv.at[3], along_z)

    blocks = []
    for s in range(2):
        table = tables_ref[s]
        top = table.astype(BF).astype(F32)
        rest = table - top
        mid = rest.astype(BF).astype(F32)
        low = rest - mid
        for part in (top, mid, low):
            for g in range(3):
                blocks.append(part[:, g * 256:(g + 1) * 256])
    matrix = jnp.concatenate(blocks, axis=0).astype(BF)
    depth = lax.broadcasted_iota(jnp.int32, (256, WT), 0)

    def some_rows(step, carry):
        found = ([], [])
        index = index_ref[pl.ds(pl.multiple_of(step * 8, 8), 8), :]
        for r in range(8):
            row = index[r:r + 1, :]
            low_part, high_part = row & 255, row >> 8
            hot = jnp.where(depth == low_part, 1.0, 0.0).astype(BF)
            picked = jnp.dot(matrix, hot, preferred_element_type=F32)
            for s in range(2):
                total = jnp.zeros((8, WT), F32)
                for g in range(3):
                    base = s * 72 + g * 8
                    value = picked[base:base + 8] + picked[base + 24:base + 32] + picked[base + 48:base + 56]
                    total = jnp.where(high_part == g, value, total)
                found[s].append(total)
        for s in range(2):
            stacked = jnp.stack(found[s], axis=0)
            bias_ref[s * 8:(s + 1) * 8, pl.ds(pl.multiple_of(step * 8, 8), 8), :] = jnp.transpose(stacked, (1, 0, 2))
        return carry

    lax.fori_loop(0, 9, some_rows, 0)
    second.wait()
    third = []
    for d in range(3):
        third.append(send(other_ref.at[0:2, x, :, y, core], other_ref.at[0:2, x, :, y, core],
                          w_send.at[4 + d], w_recv.at[4 + d], along_x[d]))
        third.append(send(other_ref.at[2:4, x, :, y, core], other_ref.at[2:4, x, :, y, core],
                          w_send.at[7 + d], w_recv.at[7 + d], along_y[d]))
    lax.fori_loop(9, WT // 8, some_rows, 0)
    for h in range(16):
        bias_ref[h] = bias_ref[h] + blocked

    for copy in pieces:
        copy.wait()

    def gather(which):
        halves = []
        for t in range(2):
            rows = []
            for di in range(2):
                rows.append(held[t, di, which * BIG:(which + 1) * BIG, :])
                base = 2 * BIG + which * SMALL
                rows.append(held[t, di, base:base + SMALL, :])
            halves.append(jnp.dot(place_ref[...], jnp.concatenate(rows, axis=0), preferred_element_type=F32))
        return jnp.concatenate(halves, axis=1)

    cells = gather(0)
    center = jnp.mean(cells, axis=1, keepdims=True)
    cells = cells - center
    spread = jnp.mean(jnp.square(cells), axis=1, keepdims=True)
    inv_std = lax.rsqrt(spread + 1e-05)
    cells = cells * inv_std
    normed[...] = cells
    normed_bf[...] = cells.astype(BF)
    inv[...] = jnp.broadcast_to(inv_std, (288, 128))
    normed_t[...] = jnp.transpose(normed_bf[...], (1, 0))
    grads[...] = gather(1).astype(BF)
    grads_t[...] = jnp.transpose(grads[...], (1, 0))

    for copy in third:
        copy.wait()
    fourth = []
    for d in range(3):
        fourth.append(send(other_ref.at[0:2, :, :, y, core], other_ref.at[0:2, :, :, y, core],
                           w_send.at[10 + d], w_recv.at[10 + d], along_y[d]))
        fourth.append(send(other_ref.at[2:4, x, :, :, core], other_ref.at[2:4, x, :, :, core],
                           w_send.at[13 + d], w_recv.at[13 + d], along_x[d]))
    for copy in own_weights:
        copy.wait()

    lane = lax.broadcasted_iota(jnp.int32, (WT, 128), 1)
    lower = lane < HD

    def split(value):
        zero = jnp.zeros_like(value)
        return jnp.concatenate([jnp.where(lower, value, zero), jnp.where(lower, zero, value)], axis=0)

    def weight(half, c):
        if half == 0:
            return (wq_ref[c] if c < 3 else wp_ref[...]).reshape(1024, 512)
        return other_ref[c].reshape(1024, 512)

    def project(half):
        for c in range(4):
            left = normed_bf if c < 3 else grads
            value = jnp.dot(left[...], weight(half, c), preferred_element_type=F32)
            value = value.astype(BF)
            if c == 0:
                value = value * jnp.asarray(0.125, BF)
            parts[c] = value

    def attend(half):
        def pair(p, carry):
            span = pl.ds(pl.multiple_of(p * 128, 128), 128)
            for w in range(2):
                rows = pl.ds(w * WT, WT)
                q, k, v, g = (parts[c, rows, span] for c in range(4))
                qq, gg = split(q), split(g)
                bias = jnp.concatenate([bias_ref[half * 8 + 2 * p], bias_ref[half * 8 + 2 * p + 1]], axis=0)
                contract = (((1,), (1,)), ((), ()))
                flip = (((0,), (0,)), ((), ()))
                scores = lax.dot_general(qq, k, contract, preferred_element_type=F32) + bias
                weights = jnp.exp(scores)
                probs = weights / jnp.sum(weights, axis=1, keepdims=True)
                probs_bf = probs.astype(BF)
                found = jnp.dot(probs_bf, v, preferred_element_type=F32)
                att[rows, span] = jnp.where(lower, found[0:WT], found[WT:]).astype(BF)
                gprobs = lax.dot_general(gg, v, contract, preferred_element_type=F32)
                dot_sum = jnp.sum(probs * gprobs, axis=1, keepdims=True)
                gscores = (probs * (gprobs - dot_sum)).astype(BF)
                gq = jnp.dot(gscores, k, preferred_element_type=F32)
                dparts[0, rows, span] = (jnp.where(lower, gq[0:WT], gq[WT:]) * 0.125).astype(BF)
                dparts[1, rows, span] = lax.dot_general(gscores, qq, flip, preferred_element_type=F32).astype(BF)
                dparts[2, rows, span] = lax.dot_general(probs_bf, gg, flip, preferred_element_type=F32).astype(BF)
            return carry

        lax.fori_loop(0, 4, pair, 0)

    def input_grad(half):
        for c in range(3):
            value = lax.dot_general(dparts[c], weight(half, c), (((1,), (1,)), ((), ())), preferred_element_type=F32)
            if half == 0 and c == 0:
                dx[...] = value
            else:
                dx[...] += value

    def weight_grad(half):
        copies = []
        for c in range(4):
            left = normed_t if c < 3 else grads_t

            def block(r, carry):
                rows = pl.ds(pl.multiple_of(r * 256, 256), 256)
                right = dparts[c] if c < 3 else att[...]
                value = jnp.dot(left[rows, :], right, preferred_element_type=F32).astype(BF)
                sums[half, c, pl.ds(r * 8, 8)] = value.reshape(8, 2, 16, 512)
                return carry

            lax.fori_loop(0, 4, block, 0)
            copies.append(send(sums.at[half, c, :, 1 - core], core_in.at[half, c],
                               r_send.at[half, c], r_recv.at[half, c], sibling))
        return copies

    def reduce_first(half, copies):
        for copy in copies:
            copy.wait()

        def add(n, carry):
            for k in range(4):
                rows = pl.ds(k * 8, 8)
                value = sums[half, n, rows, core].astype(F32) + core_in[half, n, rows].astype(F32)
                core_sum[half, n, k] = value.reshape(2, 4, 16, 512).astype(BF)
            return carry

        lax.fori_loop(0, 4, add, 0)
        stage = []
        for d in range(3):
            stage.append(send(core_sum.at[half, 0:2, (x + d + 1) % 4], xa_in.at[half, d],
                              r_send.at[half, 4 + d], r_recv.at[half, 4 + d], along_x[d]))
            stage.append(send(core_sum.at[half, 2:4, :, :, (y + d + 1) % 4], yb_in.at[half, d],
                              r_send.at[half, 7 + d], r_recv.at[half, 7 + d], along_y[d]))
        return stage

    def reduce_second(half, copies):
        for copy in copies:
            copy.wait()
        for n in range(2):
            value = core_sum[half, n, x].astype(F32)
            for d in range(3):
                value += xa_in[half, d, n].astype(F32)
            xa_sum[half, n] = value.astype(BF)
            value = core_sum[half, 2 + n, :, :, y].astype(F32)
            for d in range(3):
                value += yb_in[half, d, n].astype(F32)
            yb_sum[half, n] = value.astype(BF)
        stage = []
        for d in range(3):
            stage.append(send(xa_sum.at[half, :, :, (y + d + 1) % 4], ya_in.at[half, d],
                              r_send.at[half, 10 + d], r_recv.at[half, 10 + d], along_y[d]))
            stage.append(send(yb_sum.at[half, :, (x + d + 1) % 4], xb_in.at[half, d],
                              r_send.at[half, 13 + d], r_recv.at[half, 13 + d], along_x[d]))
        return stage

    def reduce_third(half, copies):
        for copy in copies:
            copy.wait()
        for n in range(2):
            value = xa_sum[half, n, :, y].astype(F32)
            for d in range(3):
                value += ya_in[half, d, n].astype(F32)
            z_out[half, n] = value.astype(BF)
            value = yb_sum[half, n, x].astype(F32)
            for d in range(3):
                value += xb_in[half, d, n].astype(F32)
            z_out[half, 2 + n] = value.astype(BF)
        return [send(z_out.at[half, :, 1 - zl], z_in.at[half], r_send.at[half, 16], r_recv.at[half, 16], along_z)]

    project(0)
    attend(0)
    for copy in fourth:
        copy.wait()
    fifth = send(other_ref.at[:, :, :, :, core], other_ref.at[:, :, :, :, core], w_send.at[16], w_recv.at[16], sibling)
    near = weight_grad(0)
    input_grad(0)
    fifth.wait()
    project(1)
    near = reduce_first(0, near)
    attend(1)
    near = reduce_second(0, near)
    far = weight_grad(1)
    input_grad(1)

    total = dx[...]
    mean_grad = jnp.mean(total, axis=1, keepdims=True)
    mean_cross = jnp.mean(total * normed[...], axis=1, keepdims=True)
    result = (inv[:, 0:1] * (total - mean_grad - normed[...] * mean_cross)).astype(BF)
    moved = jnp.dot(placet_ref[...], result, preferred_element_type=F32).astype(BF)
    for di in range(2):
        for t in range(2):
            back[t, di] = moved[di * PIECE:(di + 1) * PIECE, t * 512:(t + 1) * 512]

    far = reduce_first(1, far)
    spans = (pl.ds(0, BIG), pl.ds(BIG, SMALL))
    pieces = []
    for n, (di, dj, to_tp, target) in enumerate(behind):
        pieces.append(send(back.at[to_tp, di, spans[dj]], landed.at[tp, di, spans[dj]],
                           back_send.at[n], back_recv.at[n], target))
    own = pltpu.make_async_copy(back.at[tp, 0, spans[0]], landed.at[tp, 0, spans[0]], local_sem.at[3])
    own.start()
    pieces.append(own)
    near = reduce_third(0, near)
    far = reduce_second(1, far)
    far = reduce_third(1, far)
    for copy in near + far:
        copy.wait()
    for c in range(4):
        t_out[c] = (z_out[1, c, zl].astype(F32) + z_in[1, c].astype(F32)).astype(BF)
    last = send(t_out, t_in, r_send.at[0, 17], r_recv.at[0, 17], partner)
    for copy in pieces:
        copy.wait()
    last.wait()
    for c in range(4):
        total_ref[c] = z_out[0, c, zl].astype(F32) + z_in[0, c].astype(F32) + t_in[c].astype(F32)


def finish_kernel(landed, total_ref, packt_ref, tokens_ref, qkv_ref, proj_ref):
    for t in range(2):
        cells = landed[t].reshape(2 * PIECE, 512)
        moved = jnp.dot(packt_ref[...], cells, preferred_element_type=F32).astype(BF)
        if t == 0:
            tokens_ref[144:432, :] = moved
        else:
            tokens_ref[432:576, :] = moved[0:144]
            tokens_ref[0:144, :] = moved[144:288]
    qkv_ref[...] = total_ref[0:3]
    proj_ref[...] = total_ref[3]


VM = pl.BlockSpec(memory_space=pltpu.VMEM)
HB = pl.BlockSpec(memory_space=pl.ANY)
LIMIT = 60 * 1024 * 1024


def shards(tokens, w_qkv, w_proj, bias_table, bias_index, regions, out_grad):
    flat_in = tokens.reshape(576, 512)
    flat_grad = out_grad.reshape(576, 512)
    wq = w_qkv.transpose(1, 0, 2).reshape(3, 64, 16, 512)
    wp = w_proj.reshape(64, 16, 512)
    pack = jnp.asarray(PACK, BF)
    packt = jnp.asarray(np.concatenate([PACK[0].T, PACK[1].T], axis=1), BF)
    place = jnp.asarray(PLACE, BF)
    placet = jnp.asarray(PLACE.T, BF)
    dma = pltpu.SemaphoreType.DMA
    shape = jax.ShapeDtypeStruct
    vmem = pltpu.VMEM
    landed, total = pl.pallas_call(
        whole_kernel,
        out_shape=(shape((2, 2, PIECE, 512), BF), shape((4, 16, 512), F32)),
        in_specs=[VM] * 5 + [HB] * 2 + [VM] * 3,
        out_specs=(VM, VM),
        scratch_shapes=[
            vmem((3, 64, 16, 512), BF), vmem((64, 16, 512), BF),
            vmem((4, 4, 2, 4, 2, 16, 512), BF), vmem((2, 8, 768), F32),
            vmem((2, 2, 2 * PIECE, 512), BF), vmem((2, 2, 2 * PIECE, 512), BF), vmem((16, WT, WT), F32),
            vmem((288, 1024), F32), vmem((288, 1024), BF), vmem((288, 1024), BF), vmem((1024, 288), BF),
            vmem((1024, 288), BF), vmem((288, 128), F32), vmem((4, 288, 512), BF), vmem((3, 288, 512), BF),
            vmem((288, 512), BF), vmem((288, 1024), F32), vmem((2, 2, PIECE, 512), BF),
            vmem((2, 4, 32, 2, 16, 512), BF), vmem((2, 4, 32, 16, 512), BF), vmem((2, 4, 4, 2, 4, 16, 512), BF),
            vmem((2, 3, 2, 2, 4, 16, 512), BF), vmem((2, 3, 2, 4, 2, 16, 512), BF),
            vmem((2, 2, 2, 4, 16, 512), BF), vmem((2, 2, 4, 2, 16, 512), BF),
            vmem((2, 3, 2, 2, 16, 512), BF), vmem((2, 3, 2, 2, 16, 512), BF),
            vmem((2, 4, 2, 16, 512), BF), vmem((2, 4, 16, 512), BF),
            vmem((4, 16, 512), BF), vmem((4, 16, 512), BF),
            dma((7,)), dma((7,)), dma((7,)), dma((7,)), dma((17,)), dma((17,)), dma((2, 18)), dma((2, 18)), dma((4,)),
        ],
        compiler_params=pltpu.CompilerParams(collective_id=0, has_side_effects=True, vmem_limit_bytes=LIMIT),
        name="whole",
    )(flat_in, flat_grad, pack, place, placet, wq, wp, bias_table.T, bias_index, regions.transpose(1, 0, 2))

    grad_tokens, qkv_grad, proj_grad = pl.pallas_call(
        finish_kernel,
        out_shape=(shape((576, 512), BF), shape((3, 16, 512), F32), shape((16, 512), F32)),
        in_specs=[VM] * 3,
        out_specs=(VM, VM, VM),
        name="finish",
    )(landed, total, packt)
    return grad_tokens.reshape(tokens.shape), qkv_grad.transpose(1, 0, 2), proj_grad


def solution(mesh):
    in_specs = (
        P(None, "lat", "lon", "tp"),
        P(None, None, "tp"),
        P(None, "tp"),
        P(None, "tp"),
        P(),
        P(None, "lat", "lon"),
        P(None, "lat", "lon", "tp"),
    )
    out_specs = (
        P(None, "lat", "lon", "tp"),
        P(("lat", "lon"), None, "tp"),
        P(("lat", "lon"), "tp"),
    )
    return jax.shard_map(shards, mesh=mesh, in_specs=in_specs, out_specs=out_specs, check_vma=False)
```

time: 165 us -> 115 us (0.70)
  Pallas kernels: 158 us -> 114 us
  local copies, waits for them, and re-layouts: 6.15 us -> 0 us
    pallas_call x4 -> x2, Pallas kernels: 158 us -> 114 us  [the longest x1 112 us: shards(): pl.pallas_call(whole_kernel, out_shape=(shape((2, 2, PIECE, 512), BF), sh...]
    unnamed x2 -> x0, local copies, waits for them, and re-layouts: 3.24 us -> none
where the time goes in v2:
time: 115 us
  Pallas kernels  114 us (99%)
    pallas_call x1, Pallas kernels, shards(): pl.pallas_call(whole_kernel, out_shape=(shape((2, 2, PIECE, 512), BF), sh...  112 us
    pallas_call x1, Pallas kernels, shards(): pl.pallas_call(finish_kernel, out_shape=(shape((576, 512), BF), shape((3,...  2.49 us

profile of v2, /device:TPU:0, one launch (start us, length us, event | category | flops | bytes accessed | tf_op | source)
XLA Modules:
  0.0 114.9 jit_solution(15060431026796040038)
XLA Ops:
  0.6 111.7 %whole.1 = (bf16[2,2,160,512]{3,2,1,0:T(8,128)(2,1)}, f32[4,16,512]{2,1,0:T(8,128)}) custom-call(bf16[576,512]{1,0:T(8,128)(2,1)} %bitcast.12, bf16[576,512]{1,0:T(8,128)(2,1)} %bitcast.13, bf16[2,160,288]{2,1,0:T(8,128)(2,1)} %constant.8.clone.pack_ref, bf16[288,320]{1,0:T(8,128)(2,1)} %constant.10.clone.place_ref, ...), custom_call_target="tpu_custom_call" | custom-call | tf_op jit(solution)/shard_map/whole/pallas_call | solution.py:443
  112.4 2.5 %finish.1 = (bf16[576,512]{1,0:T(8,128)(2,1)}, f32[3,16,512]{2,1,0:T(8,128)}, f32[16,512]{1,0:T(8,128)}) custom-call(bf16[2,2,160,512]{3,2,1,0:T(8,128)(2,1)} %get-tuple-element.8.landed, f32[4,16,512]{2,1,0:T(8,128)} %get-tuple-element.9.total_ref, bf16[288,320]{1,0:T(8,128)(2,1)} %constant.9.clone.packt_ref), custom_call_target="tpu_custom_call" | custom-call | tf_op jit(solution)/shard_map/finish/pallas_call | solution.py:467

commit v3 on v2

v3 whole, which is shorter than its diff:
```python
import functools

import jax
import jax.numpy as jnp
import numpy as np
from jax import lax
from jax.experimental import pallas as pl
from jax.experimental.pallas import tpu as pltpu
from jax.sharding import PartitionSpec as P

HD = 64
WT = 144
BIG = 112
SMALL = 48
PIECE = BIG + SMALL
BOTH_BIG = 224
BOTH_SMALL = 80
BOTH = BOTH_BIG + BOTH_SMALL
MESH = pl.DeviceIdType.MESH
BF = jnp.bfloat16
F32 = jnp.float32
FAR = -1e30


def permutations():
    pack = np.zeros((2, BOTH, 576), np.float32)
    place = np.zeros((2, 288, 2 * BOTH), np.float32)
    leave = np.zeros((2 * PIECE, 288), np.float32)
    unpack = np.zeros((288, 2 * PIECE), np.float32)
    for di in range(2):
        for lv in range(2):
            for row in range(3):
                local = row + (3 if di == 0 else 0)
                for col in range(24):
                    cell = lv * 144 + local * 24 + col
                    shifted = (col - 6) % 24
                    window = (shifted // 12) * 144 + lv * 72 + (row + 3 * di) * 12 + shifted % 12
                    big = lv * 54 + row * 18 + col - 6
                    small = lv * 18 + row * 6 + col
                    for which in range(2):
                        spot = which * 108 + big if col >= 6 else BOTH_BIG + which * 36 + small
                        pack[di, spot, which * 288 + cell] = 1
                        place[which, window, di * BOTH + spot] = 1
                    spot = big if col >= 6 else BIG + small
                    leave[di * PIECE + spot, window] = 1
                    unpack[cell, di * PIECE + spot] = 1
    return pack, place, leave, unpack


PACK, PLACE, LEAVE, UNPACK = permutations()


def position():
    lat, lon, tp = lax.axis_index("lat"), lax.axis_index("lon"), lax.axis_index("tp")
    return lat, lon, tp


def device(lat, lon, tp):
    return {"lat": lat, "lon": lon, "tp": tp}


def neighbours():
    lat, lon, tp = position()
    x, zl, y, core = lat // 2, lat % 2, lon // 2, lon % 2
    sibling = device(lat, y * 2 + 1 - core, tp)
    along_x = [device(((x + d) % 4) * 2 + zl, lon, tp) for d in (1, 2, 3)]
    along_y = [device(lat, ((y + d) % 4) * 2 + core, tp) for d in (1, 2, 3)]
    along_z = device(x * 2 + 1 - zl, lon, tp)
    partner = device(lat, lon, 1 - tp)
    return x, zl, y, core, sibling, along_x, along_y, along_z, partner


def piece_ends(sign):
    lat, lon, tp = position()
    ends = []
    for di in range(2):
        for dj in range(2):
            for other in range(2):
                if di == 0 and dj == 0 and other == 0:
                    continue
                to_tp = 1 - tp if other else tp
                ends.append((di, dj, to_tp, device((lat + sign * di + 8) % 8, (lon + sign * dj + 8) % 8, to_tp)))
    return ends


def send(src, dst, send_sem, recv_sem, target):
    copy = pltpu.make_async_remote_copy(
        src_ref=src, dst_ref=dst, send_sem=send_sem, recv_sem=recv_sem, device_id=target, device_id_type=MESH
    )
    copy.start()
    return copy


def whole_kernel(tok_ref, grad_ref, pack_ref, place_ref, placet_ref, wq_hbm, wp_hbm, table_ref, index_ref, regions_ref,
                 landed, total_ref,
                 wq_ref, wp_ref, other_ref, tables_ref, packed, held, bias_ref,
                 normed, normed_bf, grads, normed_t, grads_t, both_x, both_g, inv, parts, dparts, dx, back,
                 *rest):
    groups, (t_out, t_in), sems = (rest[0:9], rest[9:18], rest[18:27]), rest[27:29], rest[29:]
    (piece_send, piece_recv, back_send, back_recv, w_send, w_recv, r_send, r_recv, t_send, t_recv, local_sem) = sems
    lat, lon, tp = position()
    x, zl, y, core, sibling, along_x, along_y, along_z, partner = neighbours()
    ahead, behind = piece_ends(-1), piece_ends(1)
    barrier = pltpu.get_barrier_semaphore()
    targets = [e[3] for e in ahead] + [e[3] for e in behind] + [sibling, along_z, partner] + along_x + along_y
    for target in targets:
        pl.semaphore_signal(barrier, inc=1, device_id=target, device_id_type=MESH)

    own_weights = [
        pltpu.make_async_copy(wq_hbm, wq_ref, local_sem.at[0]),
        pltpu.make_async_copy(wp_hbm, wp_ref, local_sem.at[1]),
    ]
    for copy in own_weights:
        copy.start()

    tables_ref[0] = jnp.zeros((8, 768), F32)
    tables_ref[0, :, 0:759] = table_ref[...]

    def pack(half):
        cells = []
        for ref in (tok_ref, grad_ref):
            if half == 0:
                cells.append(ref[144:432, :])
            else:
                cells.extend([ref[432:576, :], ref[0:144, :]])
        cells = jnp.concatenate(cells, axis=0)
        for di in range(2):
            packed[half, di] = jnp.dot(pack_ref[di], cells, preferred_element_type=F32).astype(BF)

    pack(0)
    pack(1)
    pl.semaphore_wait(barrier, len(targets))

    mine = (x * 4 + y) * 2 + core
    first = [
        send(wq_hbm.at[:, mine], other_ref.at[0:3, x, y, core], w_send.at[0], w_recv.at[0], partner),
        send(wp_hbm.at[mine], other_ref.at[3, x, y, core], w_send.at[1], w_recv.at[1], partner),
        send(tables_ref.at[0], tables_ref.at[1], w_send.at[2], w_recv.at[2], partner),
    ]
    spans = (pl.ds(0, BOTH_BIG), pl.ds(BOTH_BIG, BOTH_SMALL))
    pieces = []
    for n, (di, dj, to_tp, target) in enumerate(ahead):
        pieces.append(send(packed.at[to_tp, di, spans[dj]], held.at[tp, di, spans[dj]],
                           piece_send.at[n], piece_recv.at[n], target))
    own = pltpu.make_async_copy(packed.at[tp, 0, spans[0]], held.at[tp, 0, spans[0]], local_sem.at[2])
    own.start()
    pieces.append(own)

    for half in range(2):
        for c in range(4):
            for base in (288, 672):
                dparts[half, c, base:base + 96] = jnp.zeros((96, 512), BF)

    rows = lax.broadcasted_iota(jnp.int32, (WT, WT), 0) // 12
    cols = lax.broadcasted_iota(jnp.int32, (WT, WT), 1) // 12
    left = jnp.zeros((WT, WT), jnp.int32)
    right = jnp.zeros((WT, WT), jnp.int32)
    for lv in range(2):
        for row in range(6):
            value = regions_ref[row, pl.ds(2 * tp + lv, 1), 0:1]
            left = jnp.where(rows == lv * 6 + row, value, left)
            right = jnp.where(cols == lv * 6 + row, value, right)
    blocked = jnp.where(left == right, 0.0, FAR).astype(F32)

    first.pop().wait()
    blocks = []
    for s in range(2):
        table = tables_ref[s]
        top = table.astype(BF).astype(F32)
        rest = table - top
        mid = rest.astype(BF).astype(F32)
        low = rest - mid
        for part in (top, mid, low):
            for g in range(3):
                blocks.append(part[:, g * 256:(g + 1) * 256])
    matrix = jnp.concatenate(blocks, axis=0).astype(BF)
    depth = lax.broadcasted_iota(jnp.int32, (256, WT), 0)

    def some_rows(step, carry):
        found = ([], [])
        index = index_ref[pl.ds(pl.multiple_of(step * 8, 8), 8), :]
        for r in range(8):
            row = index[r:r + 1, :]
            low_part, high_part = row & 255, row >> 8
            hot = jnp.where(depth == low_part, 1.0, 0.0).astype(BF)
            picked = jnp.dot(matrix, hot, preferred_element_type=F32)
            for s in range(2):
                total = jnp.zeros((8, WT), F32)
                for g in range(3):
                    base = s * 72 + g * 8
                    value = picked[base:base + 8] + picked[base + 24:base + 32] + picked[base + 48:base + 56]
                    total = jnp.where(high_part == g, value, total)
                found[s].append(total)
        for s in range(2):
            stacked = jnp.stack(found[s], axis=0)
            bias_ref[s * 8:(s + 1) * 8, pl.ds(pl.multiple_of(step * 8, 8), 8), :] = jnp.transpose(stacked, (1, 0, 2))
        return carry

    lax.fori_loop(0, 6, some_rows, 0)
    for copy in first:
        copy.wait()

    def share(part, copies, n, target):
        copies.append(send(part, part, w_send.at[n], w_recv.at[n], target))

    third, fourth, fifth = [], [], []
    for d in range(3):
        share(other_ref.at[0:2, x, y, core], third, 3 + d, along_x[d])
        share(other_ref.at[2:4, x, y, core], third, 6 + d, along_y[d])
    lax.fori_loop(6, WT // 8, some_rows, 0)
    for h in range(16):
        bias_ref[h] = bias_ref[h] + blocked

    for copy in third + pieces:
        copy.wait()
    for d in range(3):
        share(other_ref.at[0:2, :, y, core], fourth, 9 + d, along_y[d])
        share(other_ref.at[2:4, x, :, core], fourth, 12 + d, along_x[d])
    share(other_ref.at[0:2, :, y, core], fifth, 15, sibling)
    share(other_ref.at[2:4, x, :, core], fifth, 16, sibling)

    def gather(which):
        halves = []
        for t in range(2):
            rows = held[t].reshape(2 * BOTH, 512)
            halves.append(jnp.dot(place_ref[which], rows, preferred_element_type=F32))
        return jnp.concatenate(halves, axis=1)

    cells = gather(0)
    center = jnp.mean(cells, axis=1, keepdims=True)
    cells = cells - center
    spread = jnp.mean(jnp.square(cells), axis=1, keepdims=True)
    inv_std = lax.rsqrt(spread + 1e-05)
    cells = cells * inv_std
    normed[...] = cells
    normed_bf[0:288] = cells.astype(BF)
    normed_bf[288:384] = jnp.zeros((96, 1024), BF)
    inv[...] = jnp.broadcast_to(inv_std, (288, 128))
    normed_t[...] = jnp.transpose(normed_bf[...], (1, 0)).reshape(32, 2, 16, 384)
    swaps = [send(normed_t.at[:, 1 - core], both_x.at[:, :, 384:768], t_send.at[1], t_recv.at[1], sibling)]
    grads[0:288] = gather(1).astype(BF)
    grads[288:384] = jnp.zeros((96, 1024), BF)
    grads_t[...] = jnp.transpose(grads[...], (1, 0)).reshape(32, 2, 16, 384)
    swaps.append(send(grads_t.at[:, 1 - core], both_g.at[:, :, 384:768], t_send.at[2], t_recv.at[2], sibling))
    both_x[:, :, 0:384] = normed_t[:, core]
    both_g[:, :, 0:384] = grads_t[:, core]

    for copy in own_weights:
        copy.wait()

    lane = lax.broadcasted_iota(jnp.int32, (WT, 128), 1)
    lower = lane < HD

    def split(value):
        zero = jnp.zeros_like(value)
        return jnp.concatenate([jnp.where(lower, value, zero), jnp.where(lower, zero, value)], axis=0)

    def weight(half, c):
        if half == 0:
            return (wq_ref[c] if c < 3 else wp_ref[...]).reshape(1024, 512)
        return other_ref[c].reshape(1024, 512)

    def project(half):
        for c in range(4):
            left = normed_bf if c < 3 else grads
            value = jnp.dot(left[0:288], weight(half, c), preferred_element_type=F32)
            value = value.astype(BF)
            if c == 0:
                value = value * jnp.asarray(0.125, BF)
            parts[c] = value

    def attend(half, start, stop):
        def pair(p, carry):
            span = pl.ds(pl.multiple_of(p * 128, 128), 128)
            for w in range(2):
                rows = pl.ds(w * WT, WT)
                q, k, v, g = (parts[c, rows, span] for c in range(4))
                qq, gg = split(q), split(g)
                bias = jnp.concatenate([bias_ref[half * 8 + 2 * p], bias_ref[half * 8 + 2 * p + 1]], axis=0)
                contract = (((1,), (1,)), ((), ()))
                flip = (((0,), (0,)), ((), ()))
                scores = lax.dot_general(qq, k, contract, preferred_element_type=F32) + bias
                weights = jnp.exp(scores)
                probs = weights / jnp.sum(weights, axis=1, keepdims=True)
                probs_bf = probs.astype(BF)
                found = jnp.dot(probs_bf, v, preferred_element_type=F32)
                dparts[half, 3, rows, span] = jnp.where(lower, found[0:WT], found[WT:]).astype(BF)
                gprobs = lax.dot_general(gg, v, contract, preferred_element_type=F32)
                dot_sum = jnp.sum(probs * gprobs, axis=1, keepdims=True)
                gscores = (probs * (gprobs - dot_sum)).astype(BF)
                gq = jnp.dot(gscores, k, preferred_element_type=F32)
                dparts[half, 0, rows, span] = (jnp.where(lower, gq[0:WT], gq[WT:]) * 0.125).astype(BF)
                dparts[half, 1, rows, span] = lax.dot_general(gscores, qq, flip, preferred_element_type=F32).astype(BF)
                dparts[half, 2, rows, span] = lax.dot_general(probs_bf, gg, flip, preferred_element_type=F32).astype(BF)
            return carry

        lax.fori_loop(start, stop, pair, 0)

    def input_grad(half):
        for c in range(3):
            value = lax.dot_general(dparts[half, c, 0:288], weight(half, c), (((1,), (1,)), ((), ())), preferred_element_type=F32)
            if half == 0 and c == 0:
                dx[...] = value
            else:
                dx[...] += value

    def swap(group, half, start, width):
        span = pl.ds(start, width)
        return send(dparts.at[half, :, 0:288, span], dparts.at[half, :, 384:672, span],
                    r_send.at[group, 0], r_recv.at[group, 0], sibling)

    def weight_grad(group, half, start, width, copy):
        mine, first_x, first_y = groups[group][0:3]
        span = pl.ds(start, width)
        copy.wait()
        stage = []
        for c in range(4):
            left = both_x if c < 3 else both_g
            value = jnp.dot(left[...].reshape(512, 768), dparts[half, c, :, span], preferred_element_type=F32)
            mine[c] = value.astype(BF).reshape(4, 2, 4, 16, width)
            for d in range(3):
                n = 4 + 3 * c + d
                if c % 2 == 0:
                    stage.append(send(mine.at[c, (x + d + 1) % 4], first_x.at[c // 2, d],
                                      r_send.at[group, n], r_recv.at[group, n], along_x[d]))
                else:
                    stage.append(send(mine.at[c, :, :, (y + d + 1) % 4], first_y.at[c // 2, d],
                                      r_send.at[group, n], r_recv.at[group, n], along_y[d]))
        return stage

    def reduce_second(group, copies):
        mine, first_x, first_y, mid_x, mid_y, second_x, second_y = groups[group][0:7]
        for copy in copies:
            copy.wait()
        for n in range(2):
            value = mine[2 * n, x].astype(F32)
            for d in range(3):
                value += first_x[n, d].astype(F32)
            mid_x[n] = value.astype(BF)
            value = mine[2 * n + 1, :, :, y].astype(F32)
            for d in range(3):
                value += first_y[n, d].astype(F32)
            mid_y[n] = value.astype(BF)
        stage = []
        for d in range(3):
            stage.append(send(mid_x.at[:, :, (y + d + 1) % 4], second_x.at[d],
                              r_send.at[group, 16 + d], r_recv.at[group, 16 + d], along_y[d]))
            stage.append(send(mid_y.at[:, (x + d + 1) % 4], second_y.at[d],
                              r_send.at[group, 19 + d], r_recv.at[group, 19 + d], along_x[d]))
        return stage

    def reduce_third(group, copies):
        mid_x, mid_y, second_x, second_y, z_out, z_in = groups[group][3:9]
        for copy in copies:
            copy.wait()
        for n in range(2):
            value = mid_x[n, :, y].astype(F32)
            for d in range(3):
                value += second_x[d, n].astype(F32)
            z_out[2 * n] = value.astype(BF)
            value = mid_y[n, x].astype(F32)
            for d in range(3):
                value += second_y[d, n].astype(F32)
            z_out[2 * n + 1] = value.astype(BF)
        return [send(z_out.at[:, 1 - zl], z_in, r_send.at[group, 22], r_recv.at[group, 22], along_z)]

    def reduced(group, c):
        z_out, z_in = groups[group][7:9]
        return z_out[c, zl].astype(F32) + z_in[c].astype(F32)

    project(0)
    attend(0, 0, 4)
    step = swap(0, 0, 0, 512)
    input_grad(0)
    for copy in swaps:
        copy.wait()
    stage0 = weight_grad(0, 0, 0, 512, step)
    for copy in fourth:
        copy.wait()
    for d in range(3):
        share(other_ref.at[0:2, :, (y + 3 - d) % 4, core], fifth, 17 + d, sibling)
        share(other_ref.at[2:4, (x + 3 - d) % 4, :, core], fifth, 20 + d, sibling)
    for copy in fifth:
        copy.wait()
    project(1)
    attend(1, 0, 2)
    step = swap(1, 1, 0, 256)
    stage0 = reduce_second(0, stage0)
    stage1 = weight_grad(1, 1, 0, 256, step)
    attend(1, 2, 4)
    step = swap(2, 1, 256, 256)
    stage0 = reduce_third(0, stage0)
    stage2 = weight_grad(2, 1, 256, 256, step)
    input_grad(1)

    total = dx[...]
    mean_grad = jnp.mean(total, axis=1, keepdims=True)
    mean_cross = jnp.mean(total * normed[...], axis=1, keepdims=True)
    result = (inv[:, 0:1] * (total - mean_grad - normed[...] * mean_cross)).astype(BF)
    moved = jnp.dot(placet_ref[...], result, preferred_element_type=F32).astype(BF)
    for di in range(2):
        for t in range(2):
            back[t, di] = moved[di * PIECE:(di + 1) * PIECE, t * 512:(t + 1) * 512]

    spans = (pl.ds(0, BIG), pl.ds(BIG, SMALL))
    pieces = []
    for n, (di, dj, to_tp, target) in enumerate(behind):
        pieces.append(send(back.at[to_tp, di, spans[dj]], landed.at[tp, di, spans[dj]],
                           back_send.at[n], back_recv.at[n], target))
    own = pltpu.make_async_copy(back.at[tp, 0, spans[0]], landed.at[tp, 0, spans[0]], local_sem.at[3])
    own.start()
    pieces.append(own)
    stage1 = reduce_second(1, stage1)
    stage2 = reduce_second(2, stage2)
    stage1 = reduce_third(1, stage1)
    stage2 = reduce_third(2, stage2)
    for copy in stage0 + stage1 + stage2:
        copy.wait()
    for c in range(4):
        t_out[c, :, 0:256] = reduced(1, c).astype(BF)
        t_out[c, :, 256:512] = reduced(2, c).astype(BF)
    last = send(t_out, t_in, t_send.at[0], t_recv.at[0], partner)
    for copy in pieces:
        copy.wait()
    last.wait()
    for c in range(4):
        total_ref[c] = reduced(0, c) + t_in[c].astype(F32)


def group_scratch(width):
    shapes = ((4, 4, 2, 4), (2, 3, 2, 4), (2, 3, 4, 2), (2, 2, 4), (2, 4, 2), (3, 2, 2), (3, 2, 2),
              (4, 2), (4,))
    return [pltpu.VMEM(shape + (16, width), BF) for shape in shapes]


def finish_kernel(landed, total_ref, packt_ref, tokens_ref, qkv_ref, proj_ref):
    for t in range(2):
        cells = landed[t].reshape(2 * PIECE, 512)
        moved = jnp.dot(packt_ref[...], cells, preferred_element_type=F32).astype(BF)
        if t == 0:
            tokens_ref[144:432, :] = moved
        else:
            tokens_ref[432:576, :] = moved[0:144]
            tokens_ref[0:144, :] = moved[144:288]
    qkv_ref[...] = total_ref[0:3]
    proj_ref[...] = total_ref[3]


VM = pl.BlockSpec(memory_space=pltpu.VMEM)
HB = pl.BlockSpec(memory_space=pl.ANY)
LIMIT = 60 * 1024 * 1024


def shards(tokens, w_qkv, w_proj, bias_table, bias_index, regions, out_grad):
    flat_in = tokens.reshape(576, 512)
    flat_grad = out_grad.reshape(576, 512)
    wq = w_qkv.transpose(1, 0, 2).reshape(3, 32, 32, 512)
    wp = w_proj.reshape(32, 32, 512)
    pack = jnp.asarray(PACK, BF)
    packt = jnp.asarray(UNPACK, BF)
    place = jnp.asarray(PLACE, BF)
    placet = jnp.asarray(LEAVE, BF)
    dma = pltpu.SemaphoreType.DMA
    shape = jax.ShapeDtypeStruct
    vmem = pltpu.VMEM
    landed, total = pl.pallas_call(
        whole_kernel,
        out_shape=(shape((2, 2, PIECE, 512), BF), shape((4, 16, 512), F32)),
        in_specs=[VM] * 5 + [HB] * 2 + [VM] * 3,
        out_specs=(VM, VM),
        scratch_shapes=[
            vmem((3, 32, 32, 512), BF), vmem((32, 32, 512), BF),
            vmem((4, 4, 4, 2, 32, 512), BF), vmem((2, 8, 768), F32),
            vmem((2, 2, BOTH, 512), BF), vmem((2, 2, BOTH, 512), BF), vmem((16, WT, WT), F32),
            vmem((288, 1024), F32), vmem((384, 1024), BF), vmem((384, 1024), BF),
            vmem((32, 2, 16, 384), BF), vmem((32, 2, 16, 384), BF), vmem((32, 16, 768), BF), vmem((32, 16, 768), BF),
            vmem((288, 128), F32), vmem((4, 288, 512), BF), vmem((2, 4, 768, 512), BF),
            vmem((288, 1024), F32), vmem((2, 2, PIECE, 512), BF),
            *group_scratch(512), *group_scratch(256), *group_scratch(256),
            vmem((4, 16, 512), BF), vmem((4, 16, 512), BF),
            dma((7,)), dma((7,)), dma((7,)), dma((7,)), dma((23,)), dma((23,)), dma((3, 23)), dma((3, 23)), dma((3,)), dma((3,)), dma((4,)),
        ],
        compiler_params=pltpu.CompilerParams(collective_id=0, has_side_effects=True, vmem_limit_bytes=LIMIT),
        name="whole",
    )(flat_in, flat_grad, pack, place, placet, wq, wp, bias_table.T, bias_index, regions.transpose(1, 0, 2))

    grad_tokens, qkv_grad, proj_grad = pl.pallas_call(
        finish_kernel,
        out_shape=(shape((576, 512), BF), shape((3, 16, 512), F32), shape((16, 512), F32)),
        in_specs=[VM] * 3,
        out_specs=(VM, VM, VM),
        name="finish",
    )(landed, total, packt)
    return grad_tokens.reshape(tokens.shape), qkv_grad.transpose(1, 0, 2), proj_grad


def solution(mesh):
    in_specs = (
        P(None, "lat", "lon", "tp"),
        P(None, None, "tp"),
        P(None, "tp"),
        P(None, "tp"),
        P(),
        P(None, "lat", "lon"),
        P(None, "lat", "lon", "tp"),
    )
    out_specs = (
        P(None, "lat", "lon", "tp"),
        P(("lat", "lon"), None, "tp"),
        P(("lat", "lon"), "tp"),
    )
    return jax.shard_map(shards, mesh=mesh, in_specs=in_specs, out_specs=out_specs, check_vma=False)
```

time: 115 us -> 97.5 us (0.85)
  Pallas kernels: 114 us -> 96.7 us
    pallas_call x1, Pallas kernels: 112 us -> 94.2 us  [shards(): pl.pallas_call(whole_kernel, out_shape=(shape((2, 2, PIECE, 512), BF), sh...]
where the time goes in v3:
time: 97.5 us; the launch traced here: 97.3 us
  Pallas kernels  96.7 us (99%)
    pallas_call x1, Pallas kernels, shards(): pl.pallas_call(whole_kernel, out_shape=(shape((2, 2, PIECE, 512), BF), sh...  94.2 us
    pallas_call x1, Pallas kernels, shards(): pl.pallas_call(finish_kernel, out_shape=(shape((576, 512), BF), shape((3,...  2.5 us

profile of v3, /device:TPU:0, one launch (start us, length us, event | category | flops | bytes accessed | tf_op | source)
XLA Modules:
  0.0 97.3 jit_solution(2191377427641535409)
XLA Ops:
  0.6 94.2 %whole.1 = (bf16[2,2,160,512]{3,2,1,0:T(8,128)(2,1)}, f32[4,16,512]{2,1,0:T(8,128)}) custom-call(bf16[576,512]{1,0:T(8,128)(2,1)} %bitcast.12, bf16[576,512]{1,0:T(8,128)(2,1)} %bitcast.13, bf16[2,304,576]{2,1,0:T(8,128)(2,1)} %constant.8.clone.pack_ref, bf16[2,288,608]{2,1,0:T(8,128)(2,1)} %constant.10.clone.place_ref, ...), custom_call_target="tpu_custom_call" | custom-call | tf_op jit(solution)/shard_map/whole/pallas_call | solution.py:466
  94.8 2.5 %finish.1 = (bf16[576,512]{1,0:T(8,128)(2,1)}, f32[3,16,512]{2,1,0:T(8,128)}, f32[16,512]{1,0:T(8,128)}) custom-call(bf16[2,2,160,512]{3,2,1,0:T(8,128)(2,1)} %get-tuple-element.8.landed, f32[4,16,512]{2,1,0:T(8,128)} %get-tuple-element.9.total_ref, bf16[288,320]{1,0:T(8,128)(2,1)} %constant.9.clone.packt_ref), custom_call_target="tpu_custom_call" | custom-call | tf_op jit(solution)/shard_map/finish/pallas_call | solution.py:487

commit v4 on v3

--- a/solution.py
+++ b/solution.py
@@ -96,13 +96,14 @@
                  wq_ref, wp_ref, other_ref, tables_ref, packed, held, bias_ref,
                  normed, normed_bf, grads, normed_t, grads_t, both_x, both_g, inv, parts, dparts, dx, back,
                  *rest):
-    groups, (t_out, t_in), sems = (rest[0:9], rest[9:18], rest[18:27]), rest[27:29], rest[29:]
+    groups, sems = (rest[0:18], rest[18:27], rest[27:36]), rest[36:]
     (piece_send, piece_recv, back_send, back_recv, w_send, w_recv, r_send, r_recv, t_send, t_recv, local_sem) = sems
     lat, lon, tp = position()
     x, zl, y, core, sibling, along_x, along_y, along_z, partner = neighbours()
     ahead, behind = piece_ends(-1), piece_ends(1)
     barrier = pltpu.get_barrier_semaphore()
-    targets = [e[3] for e in ahead] + [e[3] for e in behind] + [sibling, along_z, partner] + along_x + along_y
+    diagonal = device(x * 2 + 1 - zl, lon, 1 - tp)
+    targets = [diagonal] + [e[3] for e in ahead] + [e[3] for e in behind] + [sibling, along_z, partner] + along_x + along_y
     for target in targets:
         pl.semaphore_signal(barrier, inc=1, device_id=target, device_id_type=MESH)
 
@@ -127,8 +128,6 @@
         for di in range(2):
             packed[half, di] = jnp.dot(pack_ref[di], cells, preferred_element_type=F32).astype(BF)
 
-    pack(0)
-    pack(1)
     pl.semaphore_wait(barrier, len(targets))
 
     mine = (x * 4 + y) * 2 + core
@@ -138,6 +137,8 @@
         send(tables_ref.at[0], tables_ref.at[1], w_send.at[2], w_recv.at[2], partner),
     ]
     spans = (pl.ds(0, BOTH_BIG), pl.ds(BOTH_BIG, BOTH_SMALL))
+    pack(0)
+    pack(1)
     pieces = []
     for n, (di, dj, to_tp, target) in enumerate(ahead):
         pieces.append(send(packed.at[to_tp, di, spans[dj]], held.at[tp, di, spans[dj]],
@@ -196,7 +197,7 @@
             bias_ref[s * 8:(s + 1) * 8, pl.ds(pl.multiple_of(step * 8, 8), 8), :] = jnp.transpose(stacked, (1, 0, 2))
         return carry
 
-    lax.fori_loop(0, 6, some_rows, 0)
+    lax.fori_loop(0, 4, some_rows, 0)
     for copy in first:
         copy.wait()
 
@@ -205,19 +206,20 @@
 
     third, fourth, fifth = [], [], []
     for d in range(3):
-        share(other_ref.at[0:2, x, y, core], third, 3 + d, along_x[d])
-        share(other_ref.at[2:4, x, y, core], third, 6 + d, along_y[d])
-    lax.fori_loop(6, WT // 8, some_rows, 0)
+        share(other_ref.at[0:2, x, y, core], third, 3 + d, along_y[d])
+        share(other_ref.at[2:4, x, y, core], third, 6 + d, along_x[d])
+    lax.fori_loop(4, 10, some_rows, 0)
+    lax.fori_loop(10, WT // 8, some_rows, 0)
     for h in range(16):
         bias_ref[h] = bias_ref[h] + blocked
 
     for copy in third + pieces:
         copy.wait()
-    for d in range(3):
-        share(other_ref.at[0:2, :, y, core], fourth, 9 + d, along_y[d])
-        share(other_ref.at[2:4, x, :, core], fourth, 12 + d, along_x[d])
-    share(other_ref.at[0:2, :, y, core], fifth, 15, sibling)
-    share(other_ref.at[2:4, x, :, core], fifth, 16, sibling)
+    for d in (0, 2):
+        share(other_ref.at[0:2, x, :, core], fourth, 9 + d, along_x[d])
+        share(other_ref.at[2:4, :, y, core], fourth, 12 + d, along_y[d])
+    share(other_ref.at[0:2, x, :, core], fifth, 15, sibling)
+    share(other_ref.at[2:4, :, y, core], fifth, 16, sibling)
 
     def gather(which):
         halves = []
@@ -319,7 +321,7 @@
             value = jnp.dot(left[...].reshape(512, 768), dparts[half, c, :, span], preferred_element_type=F32)
             mine[c] = value.astype(BF).reshape(4, 2, 4, 16, width)
             for d in range(3):
-                n = 4 + 3 * c + d
+                n = 1 + 3 * c + d
                 if c % 2 == 0:
                     stage.append(send(mine.at[c, (x + d + 1) % 4], first_x.at[c // 2, d],
                                       r_send.at[group, n], r_recv.at[group, n], along_x[d]))
@@ -328,25 +330,25 @@
                                       r_send.at[group, n], r_recv.at[group, n], along_y[d]))
         return stage
 
+    def plus(value, others):
+        value = value.astype(F32)
+        for d in range(3):
+            value += others[d].astype(F32)
+        return value
+
     def reduce_second(group, copies):
         mine, first_x, first_y, mid_x, mid_y, second_x, second_y = groups[group][0:7]
         for copy in copies:
             copy.wait()
         for n in range(2):
-            value = mine[2 * n, x].astype(F32)
-            for d in range(3):
-                value += first_x[n, d].astype(F32)
-            mid_x[n] = value.astype(BF)
-            value = mine[2 * n + 1, :, :, y].astype(F32)
-            for d in range(3):
-                value += first_y[n, d].astype(F32)
-            mid_y[n] = value.astype(BF)
+            mid_x[n] = plus(mine[2 * n, x], first_x[n]).astype(BF)
+            mid_y[n] = plus(mine[2 * n + 1, :, :, y], first_y[n]).astype(BF)
         stage = []
         for d in range(3):
             stage.append(send(mid_x.at[:, :, (y + d + 1) % 4], second_x.at[d],
-                              r_send.at[group, 16 + d], r_recv.at[group, 16 + d], along_y[d]))
+                              r_send.at[group, 13 + d], r_recv.at[group, 13 + d], along_y[d]))
             stage.append(send(mid_y.at[:, (x + d + 1) % 4], second_y.at[d],
-                              r_send.at[group, 19 + d], r_recv.at[group, 19 + d], along_x[d]))
+                              r_send.at[group, 16 + d], r_recv.at[group, 16 + d], along_x[d]))
         return stage
 
     def reduce_third(group, copies):
@@ -354,43 +356,109 @@
         for copy in copies:
             copy.wait()
         for n in range(2):
-            value = mid_x[n, :, y].astype(F32)
+            z_out[2 * n] = plus(mid_x[n, :, y], [second_x[d, n] for d in range(3)]).astype(BF)
+            z_out[2 * n + 1] = plus(mid_y[n, x], [second_y[d, n] for d in range(3)]).astype(BF)
+        return [
+            send(z_out.at[:, zl], z_in.at[0], r_send.at[group, 19], r_recv.at[group, 19], partner),
+            send(z_out.at[:, 1 - zl], z_in.at[1], r_send.at[group, 20], r_recv.at[group, 20], diagonal),
+        ]
+
+    def early_grad(group, half, start, width, copy):
+        mine, first_x, first_y, first_z = groups[group][0:4]
+        span = pl.ds(start, width)
+        copy.wait()
+        stage = []
+        for c in (2, 3, 0, 1):
+            left = both_x if c < 3 else both_g
+            value = jnp.dot(left[...].reshape(512, 768), dparts[half, c, :, span], preferred_element_type=F32)
+            mine[c] = value.astype(BF).reshape(4, 2, 4, 16, width)
+            if c == 3:
+                stage.append(send(mine.at[2:4, :, 1 - zl], first_z, r_send.at[group, 1], r_recv.at[group, 1], along_z))
             for d in range(3):
-                value += second_x[d, n].astype(F32)
-            z_out[2 * n] = value.astype(BF)
-            value = mid_y[n, x].astype(F32)
-            for d in range(3):
-                value += second_y[d, n].astype(F32)
-            z_out[2 * n + 1] = value.astype(BF)
-        return [send(z_out.at[:, 1 - zl], z_in, r_send.at[group, 22], r_recv.at[group, 22], along_z)]
-
-    def reduced(group, c):
-        z_out, z_in = groups[group][7:9]
-        return z_out[c, zl].astype(F32) + z_in[c].astype(F32)
+                if c == 0:
+                    stage.append(send(mine.at[0, (x + d + 1) % 4], first_x.at[d],
+                                      r_send.at[group, 2 + d], r_recv.at[group, 2 + d], along_x[d]))
+                if c == 1:
+                    stage.append(send(mine.at[1, :, :, (y + d + 1) % 4], first_y.at[d],
+                                      r_send.at[group, 5 + d], r_recv.at[group, 5 + d], along_y[d]))
+        return stage
+
+    def early_second(group, copies):
+        mine, first_x, first_y, first_z, mid_x, mid_y, mid_z, second_x, second_y, second_zx, second_zy = groups[group][0:11]
+        for copy in copies:
+            copy.wait()
+        mid_x[...] = plus(mine[0, x], first_x).astype(BF)
+        mid_y[...] = plus(mine[1, :, :, y], first_y).astype(BF)
+        mid_z[...] = (mine[2:4, :, zl].astype(F32) + first_z[...].astype(F32)).astype(BF)
+        stage = []
+        for d in range(3):
+            to_x, to_y = (x + d + 1) % 4, (y + d + 1) % 4
+            for n, (src, dst, target) in enumerate((
+                (mid_z.at[0, to_x], second_zx.at[d], along_x[d]),
+                (mid_z.at[1, :, to_y], second_zy.at[d], along_y[d]),
+                (mid_x.at[:, to_y], second_x.at[d], along_y[d]),
+                (mid_y.at[to_x], second_y.at[d], along_x[d]),
+            )):
+                stage.append(send(src, dst, r_send.at[group, 8 + 4 * d + n], r_recv.at[group, 8 + 4 * d + n], target))
+        return stage
+
+    def early_third(group, copies):
+        (mid_x, mid_y, mid_z, second_x, second_y, second_zx, second_zy, z_out, z_in,
+         late_x, late_y, third_x, third_y) = groups[group][4:17]
+        for copy in copies:
+            copy.wait()
+        z_out[0] = plus(mid_x[:, y], second_x).astype(BF)
+        z_out[1] = plus(mid_y[x], second_y).astype(BF)
+        late_x[...] = plus(mid_z[0, x], second_zx).astype(BF)
+        late_y[...] = plus(mid_z[1, :, y], second_zy).astype(BF)
+        stage = [send(z_out.at[:, 1 - zl], z_in, r_send.at[group, 20], r_recv.at[group, 20], along_z)]
+        for d in range(3):
+            stage.append(send(late_x.at[(y + d + 1) % 4], third_x.at[d],
+                              r_send.at[group, 21 + d], r_recv.at[group, 21 + d], along_y[d]))
+            stage.append(send(late_y.at[(x + d + 1) % 4], third_y.at[d],
+                              r_send.at[group, 24 + d], r_recv.at[group, 24 + d], along_x[d]))
+        return stage
+
+    def early_last(group, copies):
+        z_out, z_in, late_x, late_y, third_x, third_y, done = groups[group][11:18]
+        for copy in copies:
+            copy.wait()
+        for c in range(2):
+            done[c] = z_out[c, zl].astype(F32) + z_in[c].astype(F32)
+        done[2] = plus(late_x[y], third_x)
+        done[3] = plus(late_y[x], third_y)
 
     project(0)
-    attend(0, 0, 4)
+    attend(0, 0, 2)
+    for copy in fourth:
+        copy.wait()
+    relay = []
+    for d in (0, 2):
+        from_y, from_x = (y + 3 - d) % 4, (x + 3 - d) % 4
+        part = pl.ds(d, 2)
+        share(other_ref.at[0:2, from_x, part, core], relay, 23 + d, along_x[d])
+        share(other_ref.at[2:4, part, from_y, core], relay, 24 + d, along_y[d])
+        share(other_ref.at[0:2, from_x, :, core], fifth, 17 + d, sibling)
+        share(other_ref.at[2:4, :, from_y, core], fifth, 20 + d, sibling)
+    attend(0, 2, 4)
     step = swap(0, 0, 0, 512)
     input_grad(0)
-    for copy in swaps:
-        copy.wait()
-    stage0 = weight_grad(0, 0, 0, 512, step)
-    for copy in fourth:
-        copy.wait()
-    for d in range(3):
-        share(other_ref.at[0:2, :, (y + 3 - d) % 4, core], fifth, 17 + d, sibling)
-        share(other_ref.at[2:4, (x + 3 - d) % 4, :, core], fifth, 20 + d, sibling)
+    for copy in swaps + relay:
+        copy.wait()
+    share(other_ref.at[0:2, (x + 2) % 4, :, core], fifth, 18, sibling)
+    share(other_ref.at[2:4, :, (y + 2) % 4, core], fifth, 21, sibling)
+    stage0 = early_grad(0, 0, 0, 512, step)
     for copy in fifth:
         copy.wait()
     project(1)
-    attend(1, 0, 2)
-    step = swap(1, 1, 0, 256)
-    stage0 = reduce_second(0, stage0)
-    stage1 = weight_grad(1, 1, 0, 256, step)
-    attend(1, 2, 4)
-    step = swap(2, 1, 256, 256)
-    stage0 = reduce_third(0, stage0)
-    stage2 = weight_grad(2, 1, 256, 256, step)
+    attend(1, 0, 3)
+    step = swap(1, 1, 0, 384)
+    stage1 = weight_grad(1, 1, 0, 384, step)
+    stage0 = early_second(0, stage0)
+    attend(1, 3, 4)
+    step = swap(2, 1, 384, 128)
+    stage2 = weight_grad(2, 1, 384, 128, step)
+    stage0 = early_third(0, stage0)
     input_grad(1)
 
     total = dx[...]
@@ -413,23 +481,24 @@
     stage1 = reduce_second(1, stage1)
     stage2 = reduce_second(2, stage2)
     stage1 = reduce_third(1, stage1)
+    early_last(0, stage0)
     stage2 = reduce_third(2, stage2)
-    for copy in stage0 + stage1 + stage2:
-        copy.wait()
-    for c in range(4):
-        t_out[c, :, 0:256] = reduced(1, c).astype(BF)
-        t_out[c, :, 256:512] = reduced(2, c).astype(BF)
-    last = send(t_out, t_in, t_send.at[0], t_recv.at[0], partner)
-    for copy in pieces:
-        copy.wait()
-    last.wait()
-    for c in range(4):
-        total_ref[c] = reduced(0, c) + t_in[c].astype(F32)
+    for copy in pieces + stage1 + stage2:
+        copy.wait()
+    done = groups[0][17]
+    for group, span in ((1, pl.ds(0, 384)), (2, pl.ds(384, 128))):
+        others = groups[group][8]
+        total_ref[:, :, span] = (done[:, :, span] + others[0].astype(F32) + others[1].astype(F32))
+
+
+def early_scratch(width):
+    shapes = ((4, 4, 2, 4), (3, 2, 4), (3, 4, 2), (2, 4, 4), (2, 4), (4, 2), (2, 4, 4),
+              (3, 2), (3, 2), (3, 4), (3, 4), (2, 2), (2,), (4,), (4,), (3,), (3,))
+    return [pltpu.VMEM(shape + (16, width), BF) for shape in shapes] + [pltpu.VMEM((4, 16, width), F32)]
 
 
 def group_scratch(width):
-    shapes = ((4, 4, 2, 4), (2, 3, 2, 4), (2, 3, 4, 2), (2, 2, 4), (2, 4, 2), (3, 2, 2), (3, 2, 2),
-              (4, 2), (4,))
+    shapes = ((4, 4, 2, 4), (2, 3, 2, 4), (2, 3, 4, 2), (2, 2, 4), (2, 4, 2), (3, 2, 2), (3, 2, 2), (4, 2), (2, 4))
     return [pltpu.VMEM(shape + (16, width), BF) for shape in shapes]
 
 
@@ -476,9 +545,8 @@
             vmem((32, 2, 16, 384), BF), vmem((32, 2, 16, 384), BF), vmem((32, 16, 768), BF), vmem((32, 16, 768), BF),
             vmem((288, 128), F32), vmem((4, 288, 512), BF), vmem((2, 4, 768, 512), BF),
             vmem((288, 1024), F32), vmem((2, 2, PIECE, 512), BF),
-            *group_scratch(512), *group_scratch(256), *group_scratch(256),
-            vmem((4, 16, 512), BF), vmem((4, 16, 512), BF),
-            dma((7,)), dma((7,)), dma((7,)), dma((7,)), dma((23,)), dma((23,)), dma((3, 23)), dma((3, 23)), dma((3,)), dma((3,)), dma((4,)),
+            *early_scratch(512), *group_scratch(384), *group_scratch(128),
+            dma((7,)), dma((7,)), dma((7,)), dma((7,)), dma((27,)), dma((27,)), dma((3, 27)), dma((3, 27)), dma((3,)), dma((3,)), dma((4,)),
         ],
         compiler_params=pltpu.CompilerParams(collective_id=0, has_side_effects=True, vmem_limit_bytes=LIMIT),
         name="whole",

time: 97.5 us -> 95.4 us (0.978)
  Pallas kernels: 96.7 us -> 94.6 us
    pallas_call x1, Pallas kernels: 94.2 us -> 92.1 us  [shards(): pl.pallas_call(whole_kernel, out_shape=(shape((2, 2, PIECE, 512), BF), sh...]
where the time goes in v4:
time: 95.4 us; the launch traced here: 95.2 us
  Pallas kernels  94.6 us (99%)
    pallas_call x1, Pallas kernels, shards(): pl.pallas_call(whole_kernel, out_shape=(shape((2, 2, PIECE, 512), BF), sh...  92.1 us
    pallas_call x1, Pallas kernels, shards(): pl.pallas_call(finish_kernel, out_shape=(shape((576, 512), BF), shape((3,...  2.49 us

profile of v4, /device:TPU:0, one launch (start us, length us, event | category | flops | bytes accessed | tf_op | source)
XLA Modules:
  0.0 95.2 jit_solution(10863940431246991636)
XLA Ops:
  0.6 92.1 %whole.1 = (bf16[2,2,160,512]{3,2,1,0:T(8,128)(2,1)}, f32[4,16,512]{2,1,0:T(8,128)}) custom-call(bf16[576,512]{1,0:T(8,128)(2,1)} %bitcast.12, bf16[576,512]{1,0:T(8,128)(2,1)} %bitcast.13, bf16[2,304,576]{2,1,0:T(8,128)(2,1)} %constant.8.clone.pack_ref, bf16[2,288,608]{2,1,0:T(8,128)(2,1)} %constant.10.clone.place_ref, ...), custom_call_target="tpu_custom_call" | custom-call | tf_op jit(solution)/shard_map/whole/pallas_call | solution.py:535
  92.7 2.5 %finish.1 = (bf16[576,512]{1,0:T(8,128)(2,1)}, f32[3,16,512]{2,1,0:T(8,128)}, f32[16,512]{1,0:T(8,128)}) custom-call(bf16[2,2,160,512]{3,2,1,0:T(8,128)(2,1)} %get-tuple-element.8.landed, f32[4,16,512]{2,1,0:T(8,128)} %get-tuple-element.9.total_ref, bf16[288,320]{1,0:T(8,128)(2,1)} %constant.9.clone.packt_ref), custom_call_target="tpu_custom_call" | custom-call | tf_op jit(solution)/shard_map/finish/pallas_call | solution.py:555

commit v5 on v4

--- a/solution.py
+++ b/solution.py
@@ -454,12 +454,11 @@
     attend(1, 0, 3)
     step = swap(1, 1, 0, 384)
     stage1 = weight_grad(1, 1, 0, 384, step)
-    stage0 = early_second(0, stage0)
     attend(1, 3, 4)
     step = swap(2, 1, 384, 128)
+    input_grad(1)
     stage2 = weight_grad(2, 1, 384, 128, step)
-    stage0 = early_third(0, stage0)
-    input_grad(1)
+    stage0 = early_second(0, stage0)
 
     total = dx[...]
     mean_grad = jnp.mean(total, axis=1, keepdims=True)
@@ -479,6 +478,7 @@
     own.start()
     pieces.append(own)
     stage1 = reduce_second(1, stage1)
+    stage0 = early_third(0, stage0)
     stage2 = reduce_second(2, stage2)
     stage1 = reduce_third(1, stage1)
     early_last(0, stage0)

time: 95.4 us -> 93.8 us (0.983)
  Pallas kernels: 94.6 us -> 92.8 us
    pallas_call x1, Pallas kernels: 92.1 us -> 90.3 us  [shards(): pl.pallas_call(whole_kernel, out_shape=(shape((2, 2, PIECE, 512), BF), sh...]
where the time goes in v5:
time: 93.8 us; the launch traced here: 93.5 us
  Pallas kernels  92.8 us (99%)
    pallas_call x1, Pallas kernels, shards(): pl.pallas_call(whole_kernel, out_shape=(shape((2, 2, PIECE, 512), BF), sh...  90.3 us
    pallas_call x1, Pallas kernels, shards(): pl.pallas_call(finish_kernel, out_shape=(shape((576, 512), BF), shape((3,...  2.49 us

profile of v5, /device:TPU:0, one launch (start us, length us, event | category | flops | bytes accessed | tf_op | source)
XLA Modules:
  0.0 93.5 jit_solution(10101249344862177266)
XLA Ops:
  0.6 90.3 %whole.1 = (bf16[2,2,160,512]{3,2,1,0:T(8,128)(2,1)}, f32[4,16,512]{2,1,0:T(8,128)}) custom-call(bf16[576,512]{1,0:T(8,128)(2,1)} %bitcast.12, bf16[576,512]{1,0:T(8,128)(2,1)} %bitcast.13, bf16[2,304,576]{2,1,0:T(8,128)(2,1)} %constant.8.clone.pack_ref, bf16[2,288,608]{2,1,0:T(8,128)(2,1)} %constant.10.clone.place_ref, ...), custom_call_target="tpu_custom_call" | custom-call | tf_op jit(solution)/shard_map/whole/pallas_call | solution.py:535
  91.0 2.5 %finish.1 = (bf16[576,512]{1,0:T(8,128)(2,1)}, f32[3,16,512]{2,1,0:T(8,128)}, f32[16,512]{1,0:T(8,128)}) custom-call(bf16[2,2,160,512]{3,2,1,0:T(8,128)(2,1)} %get-tuple-element.8.landed, f32[4,16,512]{2,1,0:T(8,128)} %get-tuple-element.9.total_ref, bf16[288,320]{1,0:T(8,128)(2,1)} %constant.9.clone.packt_ref), custom_call_target="tpu_custom_call" | custom-call | tf_op jit(solution)/shard_map/finish/pallas_call | solution.py:555

commit v6 on v5

--- a/solution.py
+++ b/solution.py
@@ -451,13 +451,14 @@
     for copy in fifth:
         copy.wait()
     project(1)
-    attend(1, 0, 3)
-    step = swap(1, 1, 0, 384)
-    stage1 = weight_grad(1, 1, 0, 384, step)
+    attend(1, 0, 2)
+    step = swap(1, 1, 0, 256)
+    attend(1, 2, 3)
+    stage1 = weight_grad(1, 1, 0, 256, step)
     attend(1, 3, 4)
-    step = swap(2, 1, 384, 128)
+    step = swap(2, 1, 256, 256)
     input_grad(1)
-    stage2 = weight_grad(2, 1, 384, 128, step)
+    stage2 = weight_grad(2, 1, 256, 256, step)
     stage0 = early_second(0, stage0)
 
     total = dx[...]
@@ -486,7 +487,7 @@
     for copy in pieces + stage1 + stage2:
         copy.wait()
     done = groups[0][17]
-    for group, span in ((1, pl.ds(0, 384)), (2, pl.ds(384, 128))):
+    for group, span in ((1, pl.ds(0, 256)), (2, pl.ds(256, 256))):
         others = groups[group][8]
         total_ref[:, :, span] = (done[:, :, span] + others[0].astype(F32) + others[1].astype(F32))
 
@@ -545,7 +546,7 @@
             vmem((32, 2, 16, 384), BF), vmem((32, 2, 16, 384), BF), vmem((32, 16, 768), BF), vmem((32, 16, 768), BF),
             vmem((288, 128), F32), vmem((4, 288, 512), BF), vmem((2, 4, 768, 512), BF),
             vmem((288, 1024), F32), vmem((2, 2, PIECE, 512), BF),
-            *early_scratch(512), *group_scratch(384), *group_scratch(128),
+            *early_scratch(512), *group_scratch(256), *group_scratch(256),
             dma((7,)), dma((7,)), dma((7,)), dma((7,)), dma((27,)), dma((27,)), dma((3, 27)), dma((3, 27)), dma((3,)), dma((3,)), dma((4,)),
         ],
         compiler_params=pltpu.CompilerParams(collective_id=0, has_side_effects=True, vmem_limit_bytes=LIMIT),

time: 93.8 us -> 92.1 us (0.982)
  Pallas kernels: 92.8 us -> 91.3 us
    pallas_call x1, Pallas kernels: 90.3 us -> 88.8 us  [shards(): pl.pallas_call(whole_kernel, out_shape=(shape((2, 2, PIECE, 512), BF), sh...]
where the time goes in v6:
time: 92.1 us; the launch traced here: 91.9 us
  Pallas kernels  91.3 us (99%)
    pallas_call x1, Pallas kernels, shards(): pl.pallas_call(whole_kernel, out_shape=(shape((2, 2, PIECE, 512), BF), sh...  88.8 us
    pallas_call x1, Pallas kernels, shards(): pl.pallas_call(finish_kernel, out_shape=(shape((576, 512), BF), shape((3,...  2.49 us

profile of v6, /device:TPU:0, one launch (start us, length us, event | category | flops | bytes accessed | tf_op | source)
XLA Modules:
  0.0 91.9 jit_solution(12892986927783081595)
XLA Ops:
  0.6 88.8 %whole.1 = (bf16[2,2,160,512]{3,2,1,0:T(8,128)(2,1)}, f32[4,16,512]{2,1,0:T(8,128)}) custom-call(bf16[576,512]{1,0:T(8,128)(2,1)} %bitcast.12, bf16[576,512]{1,0:T(8,128)(2,1)} %bitcast.13, bf16[2,304,576]{2,1,0:T(8,128)(2,1)} %constant.8.clone.pack_ref, bf16[2,288,608]{2,1,0:T(8,128)(2,1)} %constant.10.clone.place_ref, ...), custom_call_target="tpu_custom_call" | custom-call | tf_op jit(solution)/shard_map/whole/pallas_call | solution.py:536
  89.5 2.5 %finish.1 = (bf16[576,512]{1,0:T(8,128)(2,1)}, f32[3,16,512]{2,1,0:T(8,128)}, f32[16,512]{1,0:T(8,128)}) custom-call(bf16[2,2,160,512]{3,2,1,0:T(8,128)(2,1)} %get-tuple-element.8.landed, f32[4,16,512]{2,1,0:T(8,128)} %get-tuple-element.9.total_ref, bf16[288,320]{1,0:T(8,128)(2,1)} %constant.9.clone.packt_ref), custom_call_target="tpu_custom_call" | custom-call | tf_op jit(solution)/shard_map/finish/pallas_call | solution.py:556

commit v7 on v6

--- a/solution.py
+++ b/solution.py
@@ -479,11 +479,11 @@
     own.start()
     pieces.append(own)
     stage1 = reduce_second(1, stage1)
+    stage2 = reduce_second(2, stage2)
     stage0 = early_third(0, stage0)
-    stage2 = reduce_second(2, stage2)
     stage1 = reduce_third(1, stage1)
+    stage2 = reduce_third(2, stage2)
     early_last(0, stage0)
-    stage2 = reduce_third(2, stage2)
     for copy in pieces + stage1 + stage2:
         copy.wait()
     done = groups[0][17]

time: 92.1 us -> 91.6 us (level)
  no operation moved by 1% of the time
where the time goes in v7:
time: 91.6 us; the launch traced here: 91.4 us
  Pallas kernels  90.8 us (99%)
    pallas_call x1, Pallas kernels, shards(): pl.pallas_call(whole_kernel, out_shape=(shape((2, 2, PIECE, 512), BF), sh...  88.3 us
    pallas_call x1, Pallas kernels, shards(): pl.pallas_call(finish_kernel, out_shape=(shape((576, 512), BF), shape((3,...  2.5 us

profile of v7, /device:TPU:0, one launch (start us, length us, event | category | flops | bytes accessed | tf_op | source)
XLA Modules:
  0.0 91.4 jit_solution(8523811666646920865)
XLA Ops:
  0.6 88.3 %whole.1 = (bf16[2,2,160,512]{3,2,1,0:T(8,128)(2,1)}, f32[4,16,512]{2,1,0:T(8,128)}) custom-call(bf16[576,512]{1,0:T(8,128)(2,1)} %bitcast.12, bf16[576,512]{1,0:T(8,128)(2,1)} %bitcast.13, bf16[2,304,576]{2,1,0:T(8,128)(2,1)} %constant.8.clone.pack_ref, bf16[2,288,608]{2,1,0:T(8,128)(2,1)} %constant.10.clone.place_ref, ...), custom_call_target="tpu_custom_call" | custom-call | tf_op jit(solution)/shard_map/whole/pallas_call | solution.py:536
  88.9 2.5 %finish.1 = (bf16[576,512]{1,0:T(8,128)(2,1)}, f32[3,16,512]{2,1,0:T(8,128)}, f32[16,512]{1,0:T(8,128)}) custom-call(bf16[2,2,160,512]{3,2,1,0:T(8,128)(2,1)} %get-tuple-element.8.landed, f32[4,16,512]{2,1,0:T(8,128)} %get-tuple-element.9.total_ref, bf16[288,320]{1,0:T(8,128)(2,1)} %constant.9.clone.packt_ref), custom_call_target="tpu_custom_call" | custom-call | tf_op jit(solution)/shard_map/finish/pallas_call | solution.py:556
